TPU v7x, 128 devices: a whole 4x4x4 slice. The times are simulated.
128 devices in a mesh: expert: 16 (over z, x), helper: 8 (over y, core).
Axes of the slice: x: 4, y: 4, z: 4, core: 2. Of those that a mesh axis runs over, the one named last changes fastest.
Arguments:
- tokens: bfloat16 [8192, 4096], P(('expert', 'helper')), may hold values from -6 to 6
- expert_ids: int32 [8192, 8], P(('expert', 'helper')), may hold values from 0 to 127, all different within a row; in each aligned block of 64 rows (0 to 63, 64 to 127, ...) at most 5 rows name the same one
- gate_weights: float32 [8192, 8], P(('expert', 'helper')), may hold values from 0.05 to 1
- w_gate_up: bfloat16 [128, 4096, 2048], P(('expert', 'helper')), may hold values from -0.09375 to 0.09375
- gu_scales: float32 [128, 32, 16], P(('expert', 'helper')), may hold values from 0.5 to 2
- w_down: bfloat16 [128, 1024, 4096], P(('expert', 'helper')), may hold values from -0.1875 to 0.1875
- down_scales: float32 [128, 8, 32], P(('expert', 'helper')), may hold values from 0.5 to 2
Outputs:
- moe_out: bfloat16 [8192, 4096], P(('expert', 'helper'))
Inputs may be any that keep to these rules, and one draw needn't show every extreme that they name: `expert_ids`: each row names 8 different experts; among the 64 rows of one device no expert is named by more than 5 rows, and in every draw some expert is named by exactly 5 rows of some device.
All inputs are finite; a program needn't handle non-finite values.
Results may differ from a plain program's by a relative error of at most 0.0076.
Values may be sent and summed in bfloat16 or wider, within the bound.
No kernel may reach another device: no remote copies, remote signals or barrier semaphores. Data moves between devices by JAX's collectives and lax.ppermute only.
A program may use at most 192 MiB of HBM per device.

v0:
```python
import functools

import jax
import jax.numpy as jnp
from jax import lax
from jax.experimental import pallas as pl
from jax.experimental.pallas import tpu as pltpu
from jax.sharding import PartitionSpec as P

QBLK = 128
SLOTS = 5
ROWS = 8
EXTRA = ROWS - SLOTS
MIB = 1 << 20


def iota(shape, dim):
    return lax.broadcasted_iota(jnp.int32, shape, dim)


def slots_of(ids, experts):
    tok_rows, route_count = ids.shape
    expert_of = iota((tok_rows, experts), 1)
    hit = jnp.zeros((tok_rows, experts), jnp.float32)
    for k in range(route_count):
        hit = hit + jnp.where(ids[:, k : k + 1] == expert_of, 1.0, 0.0)
    earlier = jnp.where(iota((tok_rows, tok_rows), 0) > iota((tok_rows, tok_rows), 1), 1.0, 0.0)
    rank = jnp.dot(
        earlier.astype(jnp.bfloat16), hit.astype(jnp.bfloat16), preferred_element_type=jnp.float32
    )
    return jnp.where(hit > 0.5, rank, -1.0)


def pack_kernel(ids_ref, tok_ref, out_ref, slot_ref):
    step = pl.program_id(0)
    tok_rows, feat_width = tok_ref.shape
    block_rows, group_width = out_ref.shape
    experts = block_rows // ROWS
    parts = 1 + EXTRA
    shape = (block_rows, parts * tok_rows)
    row = iota(shape, 0) % ROWS

    @pl.when(step == 0)
    def _():
        slot = slots_of(ids_ref[...], experts).astype(jnp.bfloat16)
        repeat = jnp.where(
            iota((block_rows, experts), 0) // ROWS == iota((block_rows, experts), 1), 1.0, 0.0
        ).astype(jnp.bfloat16)
        spread = lax.dot_general(
            repeat,
            jnp.concatenate([slot] * parts, axis=0),
            (((1,), (1,)), ((), ())),
            preferred_element_type=jnp.float32,
        )
        part = iota(shape, 1) // tok_rows
        slot_ref[...] = jnp.where(jnp.maximum(row - (SLOTS - 1), 0) == part, spread, -1.0)

    want = jnp.where(row < SLOTS, row, step).astype(jnp.float32)
    chosen = jnp.where(slot_ref[...] == want, 1.0, 0.0).astype(jnp.bfloat16)
    start = pl.multiple_of(step * group_width, group_width)
    source = jnp.concatenate(
        [tok_ref[:, pl.ds(start, group_width)]]
        + [tok_ref[:, f * group_width : (f + 1) * group_width] for f in range(SLOTS, ROWS)],
        axis=0,
    )
    out_ref[...] = jnp.dot(chosen, source, preferred_element_type=jnp.float32).astype(out_ref.dtype)


def pack(tokens, expert_ids, experts):
    tok_rows, feat_width = tokens.shape
    group_width = feat_width // ROWS
    block_rows = experts * ROWS
    return pl.pallas_call(
        pack_kernel,
        grid=(SLOTS,),
        out_shape=jax.ShapeDtypeStruct((block_rows, SLOTS * group_width), tokens.dtype),
        in_specs=[
            pl.BlockSpec(expert_ids.shape, lambda i: (0, 0)),
            pl.BlockSpec(tokens.shape, lambda i: (0, 0)),
        ],
        out_specs=pl.BlockSpec((block_rows, group_width), lambda i: (0, i)),
        scratch_shapes=[pltpu.VMEM((block_rows, (1 + EXTRA) * tok_rows), jnp.float32)],
        compiler_params=pltpu.CompilerParams(vmem_limit_bytes=32 * MIB),
        name="pack",
    )(expert_ids, tokens)


def plan_kernel(ids_ref, gate_ref, out_ref):
    step = pl.program_id(0)
    tok_rows, route_count = ids_ref.shape
    block_rows = out_ref.shape[-1]
    experts = block_rows // ROWS
    gates = gate_ref[...]
    mix = gates / jnp.sum(gates, axis=1, keepdims=True)
    slot = slots_of(ids_ref[...], experts)
    expert_of = iota((tok_rows, experts), 1)
    mix_of = jnp.zeros((tok_rows, experts), jnp.float32)
    for k in range(route_count):
        mix_of = mix_of + jnp.where(ids_ref[:, k : k + 1] == expert_of, mix[:, k : k + 1], 0.0)
    high = mix_of.astype(jnp.bfloat16)
    low = (mix_of - high.astype(jnp.float32)).astype(jnp.bfloat16)
    repeat = jnp.where(
        iota((experts, block_rows), 1) // ROWS == iota((experts, block_rows), 0), 1.0, 0.0
    ).astype(jnp.bfloat16)
    spread = jnp.dot(slot.astype(jnp.bfloat16), repeat, preferred_element_type=jnp.float32)
    row = iota((tok_rows, block_rows), 1) % ROWS
    for half, piece in enumerate((high, low)):
        weight = jnp.dot(piece, repeat, preferred_element_type=jnp.float32)
        for part in range(1 + EXTRA):
            if part == 0:
                keep = (row < SLOTS) & (spread == row.astype(jnp.float32))
            else:
                keep = (row == SLOTS - 1 + part) & (spread == step.astype(jnp.float32))
            first = (half * (1 + EXTRA) + part) * tok_rows
            out_ref[0, first : first + tok_rows, :] = jnp.where(keep, weight, 0.0).astype(jnp.bfloat16)


def plan(expert_ids, gate_weights, experts):
    tok_rows = expert_ids.shape[0]
    shape = (2 * (1 + EXTRA) * tok_rows, experts * ROWS)
    return pl.pallas_call(
        plan_kernel,
        grid=(SLOTS,),
        out_shape=jax.ShapeDtypeStruct((SLOTS,) + shape, jnp.bfloat16),
        in_specs=[
            pl.BlockSpec(expert_ids.shape, lambda i: (0, 0)),
            pl.BlockSpec(gate_weights.shape, lambda i: (0, 0)),
        ],
        out_specs=pl.BlockSpec((1,) + shape, lambda i: (i, 0, 0)),
        compiler_params=pltpu.CompilerParams(vmem_limit_bytes=32 * MIB),
        cost_estimate=pl.CostEstimate(flops=10**9, bytes_accessed=6 * 10**6, transcendentals=0),
        name="plan",
    )(expert_ids, gate_weights)


def dequant_kernel(scale_ref, weight_ref, out_ref):
    row_blocks, col_blocks = (n // QBLK for n in weight_ref.shape)
    first_row = pl.program_id(0) * row_blocks
    first_col = pl.program_id(1) * col_blocks
    for i in range(row_blocks):
        for j in range(col_blocks):
            here = (slice(i * QBLK, (i + 1) * QBLK), slice(j * QBLK, (j + 1) * QBLK))
            scale = scale_ref[first_row + i, first_col + j]
            out_ref[here] = (weight_ref[here].astype(jnp.float32) * scale).astype(out_ref.dtype)


def dequant(weight, scales, block, place):
    row_count, col_count = weight.shape
    return pl.pallas_call(
        dequant_kernel,
        grid=(row_count // block[0], col_count // block[1]),
        out_shape=jax.ShapeDtypeStruct(weight.shape, weight.dtype),
        in_specs=[
            pl.BlockSpec(memory_space=pltpu.SMEM),
            pl.BlockSpec(block, lambda i, j: (i, j)),
        ],
        out_specs=pl.BlockSpec(block, lambda i, j: (i, place(j))),
        compiler_params=pltpu.CompilerParams(vmem_limit_bytes=32 * MIB),
        cost_estimate=pl.CostEstimate(
            flops=row_count * col_count, bytes_accessed=4 * row_count * col_count, transcendentals=0
        ),
        name="dequant",
    )(scales, weight)


def expert_kernel(
    steps_up, sources, in_ref, gu_ref, down_ref, out_ref, x_ref, hidden_ref, extra_ref
):
    step = pl.program_id(0)
    group_width = out_ref.shape[1]
    hidden_tile = gu_ref.shape[1] // 2
    span = sources * ROWS
    kept = sources * SLOTS
    runs = in_ref.shape[0] // span

    def turned(back):
        to, come = iota((span, span), 1 if back else 0), iota((span, span), 0 if back else 1)
        same = (to // sources == come % ROWS) & (to % sources == come // ROWS)
        return jnp.where(same, 1.0, 0.0).astype(jnp.bfloat16)

    @pl.when(step == 0)
    def _():
        order = turned(False)
        for run in range(runs):
            for group in range(SLOTS):
                cols = slice(group * group_width, (group + 1) * group_width)
                moved = jnp.dot(
                    order,
                    in_ref[run * span : (run + 1) * span, cols],
                    preferred_element_type=jnp.float32,
                ).astype(x_ref.dtype)
                for row in range(ROWS):
                    slot, feature = (row, group) if row < SLOTS else (group, row)
                    first = run * kept + slot * sources
                    x_ref[
                        first : first + sources, feature * group_width : (feature + 1) * group_width
                    ] = moved[row * sources : (row + 1) * sources]

    @pl.when(step < steps_up)
    def _():
        pre = jnp.dot(x_ref[...], gu_ref[...], preferred_element_type=jnp.float32)
        gate, up = pre[:, :hidden_tile], pre[:, hidden_tile:]
        start = pl.multiple_of(step * hidden_tile, hidden_tile)
        hidden_ref[:, pl.ds(start, hidden_tile)] = (gate / (1.0 + jnp.exp(-gate)) * up).astype(
            hidden_ref.dtype
        )

    def product():
        return jnp.dot(
            hidden_ref[...], down_ref[...], preferred_element_type=jnp.float32
        ).astype(jnp.bfloat16)

    @pl.when((step >= steps_up) & (step < steps_up + EXTRA))
    def _():
        extra_ref[step - steps_up] = product()

    @pl.when(step >= steps_up + EXTRA)
    def _():
        result = product()
        group = step - (steps_up + EXTRA)
        order = turned(True)
        for run in range(runs):
            start = pl.multiple_of(run * kept + group * sources, sources)
            gathered = jnp.concatenate(
                [result[run * kept : (run + 1) * kept]]
                + [extra_ref[i, pl.ds(start, sources), :] for i in range(EXTRA)],
                axis=0,
            )
            out_ref[run * span : (run + 1) * span, :] = jnp.dot(
                order, gathered, preferred_element_type=jnp.float32
            ).astype(out_ref.dtype)


def expert(arrived, gate_up, down, hidden_tile):
    block_rows, packed_width = arrived.shape
    feat_width, hidden_width = gate_up.shape[0], down.shape[0]
    group_width = feat_width // ROWS
    live_rows = block_rows // ROWS * SLOTS
    steps_up = hidden_width // hidden_tile
    last_up = steps_up - 1

    def feature(i):
        return (jnp.maximum(i - steps_up, 0) + SLOTS) % ROWS

    return pl.pallas_call(
        functools.partial(expert_kernel, steps_up, 256 // ROWS),
        grid=(steps_up + ROWS,),
        out_shape=jax.ShapeDtypeStruct(arrived.shape, arrived.dtype),
        in_specs=[
            pl.BlockSpec(arrived.shape, lambda i: (0, 0)),
            pl.BlockSpec((feat_width, 2 * hidden_tile), lambda i: (0, jnp.minimum(i, last_up))),
            pl.BlockSpec((hidden_width, group_width), lambda i: (0, feature(i))),
        ],
        out_specs=pl.BlockSpec(
            (block_rows, group_width), lambda i: (0, jnp.maximum(i - steps_up - EXTRA, 0))
        ),
        scratch_shapes=[
            pltpu.VMEM((live_rows, feat_width), jnp.bfloat16),
            pltpu.VMEM((live_rows, hidden_width), jnp.bfloat16),
            pltpu.VMEM((EXTRA, live_rows, group_width), jnp.bfloat16),
        ],
        compiler_params=pltpu.CompilerParams(vmem_limit_bytes=56 * MIB),
        cost_estimate=pl.CostEstimate(
            flops=2 * live_rows * 3 * feat_width * hidden_width,
            bytes_accessed=6 * feat_width * hidden_width + 4 * block_rows * packed_width,
            transcendentals=live_rows * hidden_width,
        ),
        name="expert",
    )(arrived, gate_up, down)


def combine_kernel(weight_ref, in_ref, out_ref, total_ref):
    step = pl.program_id(0)
    tok_rows = out_ref.shape[0]
    group_width = in_ref.shape[1]
    half = weight_ref.shape[1] // 2
    both = jnp.dot(weight_ref[0], in_ref[...], preferred_element_type=jnp.float32)
    part = both[:half] + both[half:]
    start = pl.multiple_of(step * group_width, group_width)
    out_ref[:, pl.ds(start, group_width)] = part[:tok_rows].astype(out_ref.dtype)

    @pl.when(step == 0)
    def _():
        total_ref[...] = part[tok_rows:]

    @pl.when(step > 0)
    def _():
        total_ref[...] += part[tok_rows:]

    @pl.when(step == SLOTS - 1)
    def _():
        for i in range(EXTRA):
            cols = slice((SLOTS + i) * group_width, (SLOTS + i + 1) * group_width)
            out_ref[:, cols] = total_ref[i * tok_rows : (i + 1) * tok_rows].astype(out_ref.dtype)


def combine(weights, returned, out_shape):
    group_width = out_shape.shape[1] // ROWS
    return pl.pallas_call(
        combine_kernel,
        grid=(SLOTS,),
        out_shape=out_shape,
        in_specs=[
            pl.BlockSpec((1,) + weights.shape[1:], lambda i: (i, 0, 0)),
            pl.BlockSpec((returned.shape[0], group_width), lambda i: (0, i)),
        ],
        out_specs=pl.BlockSpec(out_shape.shape, lambda i: (0, 0)),
        scratch_shapes=[pltpu.VMEM((EXTRA * out_shape.shape[0], group_width), jnp.float32)],
        compiler_params=pltpu.CompilerParams(vmem_limit_bytes=32 * MIB),
        name="combine",
    )(weights, returned)


def exchange(blocks, experts):
    shape = blocks.shape
    moved = lax.all_to_all(
        blocks.reshape(experts, ROWS, shape[1]),
        ("expert", "helper"),
        split_axis=0,
        concat_axis=0,
        tiled=True,
    )
    return moved.reshape(shape)


def shards(tokens, expert_ids, gate_weights, w_gate_up, gu_scales, w_down, down_scales):
    experts = lax.axis_size("expert") * lax.axis_size("helper")
    hidden_width = w_down.shape[1]
    tile = 256
    tiles = hidden_width // tile
    arrived = exchange(pack(tokens, expert_ids, experts), experts)
    gate_up = dequant(
        w_gate_up[0], gu_scales[0], (1024, tile), lambda j: 2 * (j % tiles) + j // tiles
    )
    down = dequant(w_down[0], down_scales[0], (256, 1024), lambda j: j)
    weights = plan(expert_ids, gate_weights, experts)
    returned = exchange(expert(arrived, gate_up, down, tile), experts)
    return combine(weights, returned, jax.ShapeDtypeStruct(tokens.shape, tokens.dtype))


def solution(mesh):
    rows = ("expert", "helper")
    placed = (P(rows, None),) * 3 + (P(rows, None, None),) * 4
    return jax.shard_map(
        shards, mesh=mesh, in_specs=placed, out_specs=P(rows, None), check_vma=False
    )
```

profile of v0, /device:TPU:1, one launch (start us, length us, event | category | flops | bytes accessed | tf_op | source)
XLA Modules:
  0.0 190.9 jit_solution(16273001744360880866)
XLA Ops:
  0.0 0.8 copy.8.ids_ref
  0.8 0.0 copy-start.6
  0.8 1.0 copy-done.6
  1.8 3.3 %pack.1 = bf16[1024,2560]{1,0:T(8,128)(2,1)S(1)} custom-call(s32[64,8]{1,0:T(8,128)S(1)} %copy.8.ids_ref, bf16[64,4096]{1,0:T(8,128)(2,1)S(1)} %copy-done.6), custom_call_target="tpu_custom_call" | custom-call | tf_op jit(solution)/shard_map/pack/pallas_call | solution.py:73
  5.1 0.0 copy-start
  5.1 2.4 %copy-done = bf16[1024,2560]{1,0:T(8,128)(2,1)} copy-done((bf16[1024,2560]{1,0:T(8,128)(2,1)}, bf16[1024,2560]{1,0:T(8,128)(2,1)S(1)}, u32[]{:S(2)}) %copy-start) | copy-done | bytes 5242904
  7.5 0.0 copy-start.8
  7.5 0.0 copy-start.7
  7.5 11.9 %all-to-all-start = ((bf16[128,8,2560]{2,1,0:T(8,128)(2,1)}), bf16[128,8,2560]{2,1,0:T(8,128)(2,1)}, u32[]{:S(2)}, u32[]{:S(2)}) async-start(bf16[128,8,2560]{2,1,0:T(8,128)(2,1)} %bitcast.8), calls=%async_computation | async-start | bytes 10485760 | tf_op jit(solution)/shard_map/all_to_all | solution.py:316
  19.4 0.0 copy-done.8
  19.4 0.1 copy.11
  19.5 0.0 copy-done.7
  19.5 0.0 copy-start.4
  19.5 3.4 %copy-done.4 = bf16[1,1024,4096]{2,1,0:T(8,128)(2,1)S(1)} copy-done((bf16[1,1024,4096]{2,1,0:T(8,128)(2,1)S(1)}, bf16[1,1024,4096]{2,1,0:T(8,128)(2,1)}, u32[]{:S(2)}) %copy-start.4) | copy-done | bytes 8388632
  22.9 4.4 %dequant.3.down_ref = bf16[1024,4096]{1,0:T(8,128)(2,1)S(1)} custom-call(f32[8,32]{1,0:T(8,128)S(1)} %bitcast.11, bf16[1024,4096]{1,0:T(8,128)(2,1)S(1)} %bitcast.9), custom_call_target="tpu_custom_call" | custom-call | flops 4194304 | bytes 16777216 | tf_op jit(solution)/shard_map/dequant/pallas_call | solution.py:149
  27.4 0.0 copy-start.5
  27.4 3.2 %copy-done.5 = bf16[1024,4096]{1,0:T(8,128)(2,1)} copy-done((bf16[1024,4096]{1,0:T(8,128)(2,1)}, bf16[1024,4096]{1,0:T(8,128)(2,1)S(1)}, u32[]{:S(2)}) %copy-start.5) | copy-done | bytes 8388632
  30.6 20.9 %dequant.2.gu_ref = bf16[4096,2048]{1,0:T(8,128)(2,1)S(1)} custom-call(f32[32,16]{1,0:T(8,128)S(1)} %bitcast.10, bf16[4096,2048]{1,0:T(8,128)(2,1)} %bitcast.12), custom_call_target="tpu_custom_call" | custom-call | flops 8388608 | bytes 33554432 | tf_op jit(solution)/shard_map/dequant/pallas_call | solution.py:149
  51.5 0.0 copy-start.3
  51.5 5.7 %copy-done.3 = bf16[4096,2048]{1,0:T(8,128)(2,1)} copy-done((bf16[4096,2048]{1,0:T(8,128)(2,1)}, bf16[4096,2048]{1,0:T(8,128)(2,1)S(1)}, u32[]{:S(2)}) %copy-start.3) | copy-done | bytes 16777240
  57.2 26.3 %all-to-all-done = bf16[128,8,2560]{2,1,0:T(8,128)(2,1)} async-done(((bf16[128,8,2560]{2,1,0:T(8,128)(2,1)}), bf16[128,8,2560]{2,1,0:T(8,128)(2,1)}, u32[]{:S(2)}, u32[]{:S(2)}) %all-to-all-start) | async-done | bytes 5242912 | tf_op jit(solution)/shard_map/all_to_all | solution.py:316
  83.5 28.4 %expert.1 = bf16[1024,2560]{1,0:T(8,128)(2,1)} custom-call(bf16[1024,2560]{1,0:T(8,128)(2,1)} %bitcast.1.in_ref, bf16[4096,2048]{1,0:T(8,128)(2,1)} %copy-done.3, bf16[1024,4096]{1,0:T(8,128)(2,1)} %copy-done.5), custom_call_target="tpu_custom_call" | custom-call | flops 16106127360 | bytes 35651584 | tf_op jit(solution)/shard_map/expert/pallas_call | solution.py:245
  111.9 0.0 copy-start.9
  111.9 5.5 %all-to-all-start.1 = ((bf16[128,8,2560]{2,1,0:T(8,128)(2,1)}), bf16[128,8,2560]{2,1,0:T(8,128)(2,1)}, u32[]{:S(2)}, u32[]{:S(2)}) async-start(bf16[128,8,2560]{2,1,0:T(8,128)(2,1)} %bitcast.13), calls=%async_computation.1 | async-start | bytes 10485760 | tf_op jit(solution)/shard_map/all_to_all | solution.py:316
  117.5 0.0 copy-done.9
  117.5 0.1 copy.9.gate_ref
  117.6 3.7 %plan.1.weight_ref = bf16[5,512,1024]{2,1,0:T(8,128)(2,1)S(1)} custom-call(s32[64,8]{1,0:T(8,128)S(1)} %copy.8.ids_ref, f32[64,8]{1,0:T(8,128)S(1)} %copy.9.gate_ref), custom_call_target="tpu_custom_call" | custom-call | flops 1000000000 | bytes 6000000 | tf_op jit(solution)/shard_map/plan/pallas_call | solution.py:121
  121.2 0.0 copy-start.1
  121.3 2.3 %copy-done.1 = bf16[5,512,1024]{2,1,0:T(8,128)(2,1)} copy-done((bf16[5,512,1024]{2,1,0:T(8,128)(2,1)}, bf16[5,512,1024]{2,1,0:T(8,128)(2,1)S(1)}, u32[]{:S(2)}) %copy-start.1) | copy-done | bytes 5242904
  123.6 58.1 %all-to-all-done.1 = bf16[128,8,2560]{2,1,0:T(8,128)(2,1)} async-done(((bf16[128,8,2560]{2,1,0:T(8,128)(2,1)}), bf16[128,8,2560]{2,1,0:T(8,128)(2,1)}, u32[]{:S(2)}, u32[]{:S(2)}) %all-to-all-start.1) | async-done | bytes 5242912 | tf_op jit(solution)/shard_map/all_to_all | solution.py:316
  181.7 0.0 copy-start.2
  181.7 2.5 %copy-done.2 = bf16[5,512,1024]{2,1,0:T(8,128)(2,1)S(1)} copy-done((bf16[5,512,1024]{2,1,0:T(8,128)(2,1)S(1)}, bf16[5,512,1024]{2,1,0:T(8,128)(2,1)}, u32[]{:S(2)}) %copy-start.2) | copy-done | bytes 5242904
  184.2 6.7 %combine.1 = bf16[64,4096]{1,0:T(8,128)(2,1)} custom-call(bf16[5,512,1024]{2,1,0:T(8,128)(2,1)S(1)} %copy-done.2, bf16[1024,2560]{1,0:T(8,128)(2,1)} %bitcast.7.in_ref), custom_call_target="tpu_custom_call" | custom-call | tf_op jit(solution)/shard_map/combine/pallas_call | solution.py:299
Async XLA Ops:
  0.8 1.0 copy-start.6
  5.1 2.4 %copy-start = (bf16[1024,2560]{1,0:T(8,128)(2,1)}, bf16[1024,2560]{1,0:T(8,128)(2,1)S(1)}, u32[]{:S(2)}) copy-start(bf16[1024,2560]{1,0:T(8,128)(2,1)S(1)} %pack.1) | copy-start | bytes 15728644
  7.5 11.9 %copy-start.8 = (f32[1,32,16]{1,2,0:T(8,128)S(1)}, f32[1,32,16]{1,2,0:T(8,128)}, u32[]{:S(2)}) copy-start(f32[1,32,16]{1,2,0:T(8,128)} %param.11) | copy-start | bytes 6148
  7.5 12.0 %copy-start.7 = (f32[1,8,32]{2,1,0:T(8,128)S(1)}, f32[1,8,32]{2,1,0:T(8,128)}, u32[]{:S(2)}) copy-start(f32[1,8,32]{2,1,0:T(8,128)} %param.13) | copy-start | bytes 3076
  7.5 76.0 %all-to-all-start = ((bf16[128,8,2560]{2,1,0:T(8,128)(2,1)}), bf16[128,8,2560]{2,1,0:T(8,128)(2,1)}, u32[]{:S(2)}, u32[]{:S(2)}) async-start(bf16[128,8,2560]{2,1,0:T(8,128)(2,1)} %bitcast.8), calls=%async_computation | async-start | bytes 10485760 | tf_op jit(solution)/shard_map/all_to_all | solution.py:316
  19.5 3.4 %copy-start.4 = (bf16[1,1024,4096]{2,1,0:T(8,128)(2,1)S(1)}, bf16[1,1024,4096]{2,1,0:T(8,128)(2,1)}, u32[]{:S(2)}) copy-start(bf16[1,1024,4096]{2,1,0:T(8,128)(2,1)} %param.12) | copy-start | bytes 25165828
  27.4 3.2 %copy-start.5 = (bf16[1024,4096]{1,0:T(8,128)(2,1)}, bf16[1024,4096]{1,0:T(8,128)(2,1)S(1)}, u32[]{:S(2)}) copy-start(bf16[1024,4096]{1,0:T(8,128)(2,1)S(1)} %dequant.3.down_ref) | copy-start | bytes 25165828
  51.5 5.7 %copy-start.3 = (bf16[4096,2048]{1,0:T(8,128)(2,1)}, bf16[4096,2048]{1,0:T(8,128)(2,1)S(1)}, u32[]{:S(2)}) copy-start(bf16[4096,2048]{1,0:T(8,128)(2,1)S(1)} %dequant.2.gu_ref) | copy-start | bytes 50331652
  111.9 5.5 %copy-start.9 = (f32[64,8]{0,1:T(8,128)S(1)}, f32[64,8]{0,1:T(8,128)}, u32[]{:S(2)}) copy-start(f32[64,8]{0,1:T(8,128)} %param.9) | copy-start | bytes 6148
  111.9 69.8 %all-to-all-start.1 = ((bf16[128,8,2560]{2,1,0:T(8,128)(2,1)}), bf16[128,8,2560]{2,1,0:T(8,128)(2,1)}, u32[]{:S(2)}, u32[]{:S(2)}) async-start(bf16[128,8,2560]{2,1,0:T(8,128)(2,1)} %bitcast.13), calls=%async_computation.1 | async-start | bytes 10485760 | tf_op jit(solution)/shard_map/all_to_all | solution.py:316
  121.2 2.3 %copy-start.1 = (bf16[5,512,1024]{2,1,0:T(8,128)(2,1)}, bf16[5,512,1024]{2,1,0:T(8,128)(2,1)S(1)}, u32[]{:S(2)}) copy-start(bf16[5,512,1024]{2,1,0:T(8,128)(2,1)S(1)} %plan.1.weight_ref) | copy-start | bytes 15728644
  181.7 2.5 %copy-start.2 = (bf16[5,512,1024]{2,1,0:T(8,128)(2,1)S(1)}, bf16[5,512,1024]{2,1,0:T(8,128)(2,1)}, u32[]{:S(2)}) copy-start(bf16[5,512,1024]{2,1,0:T(8,128)(2,1)} %copy-done.1) | copy-start | bytes 15728644
where the time goes:
time: 192 us; the launch traced here: 191 us
  waiting for transfers between devices  84.4 us (44%)
  Pallas kernels  67.4 us (35%)
  local copies, waits for them, and re-layouts  21.5 us (11%)
  starting transfers between devices  17.4 us (9%)
    all_to_all x2, waiting for transfers between devices, exchange(): lax.all_to_all(blocks.reshape(experts, ROWS, shape[1]), ('expert', 'helpe...  84.4 us
    pallas_call x1, Pallas kernels, expert(): pl.pallas_call(functools.partial(expert_kernel, steps_up, 256 // ROWS), g...  28.4 us
    pallas_call x2, Pallas kernels, dequant(): pl.pallas_call(dequant_kernel, grid=(row_count // block[0], col_count //...  25.3 us
    unnamed x23, local copies, waits for them, and re-layouts  21.5 us
    all_to_all x2, starting transfers between devices, exchange(): lax.all_to_all(blocks.reshape(experts, ROWS, shape[1]), ('expert', 'helpe...  17.4 us
    pallas_call x1, Pallas kernels, combine(): pl.pallas_call(combine_kernel, grid=(SLOTS,), out_shape=out_shape, in_spe...  6.73 us
  transfers between devices with their start and end apart: 2, of which 2 were waited for; matrix products, arithmetic and copies ran while one was open for 0% of the time, Pallas kernels for 15%

commit v1 on v0

v1 whole, which is shorter than its diff:
```python
import functools

import jax
import jax.numpy as jnp
from jax import lax
from jax.experimental import pallas as pl
from jax.experimental.pallas import tpu as pltpu
from jax.sharding import PartitionSpec as P

QBLK = 128
SLOTS = 5
ROWS = 8
EXTRA = ROWS - SLOTS
MIB = 1 << 20


def iota(shape, dim):
    return lax.broadcasted_iota(jnp.int32, shape, dim)


def slots_of(ids, experts):
    tok_rows, route_count = ids.shape
    expert_of = iota((tok_rows, experts), 1)
    hit = jnp.zeros((tok_rows, experts), jnp.float32)
    for k in range(route_count):
        hit = hit + jnp.where(ids[:, k : k + 1] == expert_of, 1.0, 0.0)
    earlier = jnp.where(iota((tok_rows, tok_rows), 0) > iota((tok_rows, tok_rows), 1), 1.0, 0.0)
    rank = jnp.dot(
        earlier.astype(jnp.bfloat16), hit.astype(jnp.bfloat16), preferred_element_type=jnp.float32
    )
    return jnp.where(hit > 0.5, rank, -1.0)


def slots_for(ids, experts):
    route_count, tok_rows = ids.shape
    expert_of = iota((experts, tok_rows), 0)
    hit = jnp.zeros((experts, tok_rows), jnp.float32)
    for k in range(route_count):
        hit = hit + jnp.where(ids[k : k + 1, :] == expert_of, 1.0, 0.0)
    earlier = jnp.where(iota((tok_rows, tok_rows), 0) < iota((tok_rows, tok_rows), 1), 1.0, 0.0)
    rank = jnp.dot(
        hit.astype(jnp.bfloat16), earlier.astype(jnp.bfloat16), preferred_element_type=jnp.float32
    )
    return jnp.where(hit > 0.5, rank, -1.0)


ALWAYS = 99.0


def pack_kernel(ids_ref, given_ref, out_ref, tok_ref, block_ref, slot_ref, tok_sem, out_sem):
    tok_rows, feat_width = tok_ref.shape
    group_width = feat_width // ROWS
    block_rows = block_ref.shape[0]
    experts = block_rows // ROWS
    parts = 1 + EXTRA
    fetch = pltpu.make_async_copy(given_ref, tok_ref, tok_sem)
    fetch.start()

    slot = slots_for(ids_ref[...], experts).astype(jnp.bfloat16)
    repeat = jnp.where(
        iota((block_rows, experts), 0) // ROWS == iota((block_rows, experts), 1), 1.0, 0.0
    ).astype(jnp.bfloat16)
    spread = jnp.dot(
        repeat, jnp.concatenate([slot] * parts, axis=1), preferred_element_type=jnp.float32
    )
    shape = (block_rows, parts * tok_rows)
    row = iota(shape, 0) % ROWS
    part = iota(shape, 1) // tok_rows
    own = (part == 0) & (row.astype(jnp.float32) == spread) & (row < SLOTS)
    shared = (part > 0) & (row == SLOTS - 1 + part)
    slot_ref[...] = jnp.where(own, ALWAYS, jnp.where(shared, spread, -1.0))
    fetch.wait()

    def group(g):
        return slice(g * group_width, (g + 1) * group_width)

    writes = []
    for g in range(SLOTS):
        code = slot_ref[...]
        chosen = jnp.where((code == ALWAYS) | (code == float(g)), 1.0, 0.0).astype(jnp.bfloat16)
        source = jnp.concatenate(
            [tok_ref[:, group(f)] for f in (g, *range(SLOTS, ROWS))], axis=0
        )
        block_ref[:, group(g)] = jnp.dot(
            chosen, source, preferred_element_type=jnp.float32
        ).astype(block_ref.dtype)
        writes.append(
            pltpu.make_async_copy(block_ref.at[:, group(g)], out_ref.at[:, group(g)], out_sem.at[g])
        )
        writes[-1].start()
    for write in writes:
        write.wait()


def pack(tokens, expert_ids, experts):
    tok_rows, feat_width = tokens.shape
    shape = (experts * ROWS, feat_width // ROWS * SLOTS)
    return pl.pallas_call(
        pack_kernel,
        out_shape=pltpu.HBM(shape, tokens.dtype),
        in_specs=[pl.BlockSpec(memory_space=pltpu.VMEM), pl.BlockSpec(memory_space=pl.ANY)],
        out_specs=pl.BlockSpec(memory_space=pl.ANY),
        scratch_shapes=[
            pltpu.VMEM(tokens.shape, tokens.dtype),
            pltpu.VMEM(shape, tokens.dtype),
            pltpu.VMEM((shape[0], (1 + EXTRA) * tok_rows), jnp.float32),
            pltpu.SemaphoreType.DMA,
            pltpu.SemaphoreType.DMA((SLOTS,)),
        ],
        compiler_params=pltpu.CompilerParams(vmem_limit_bytes=32 * MIB),
        name="pack",
    )(expert_ids.T, pltpu.with_memory_space_constraint(tokens, pltpu.HBM))


def plan_kernel(ids_ref, gate_ref, slot_ref, mix_ref):
    tok_rows, route_count = ids_ref.shape
    block_rows = slot_ref.shape[1]
    experts = block_rows // ROWS
    gates = gate_ref[...]
    mix = gates / jnp.sum(gates, axis=1, keepdims=True)
    slot = slots_of(ids_ref[...], experts)
    expert_of = iota((tok_rows, experts), 1)
    mix_of = jnp.zeros((tok_rows, experts), jnp.float32)
    for k in range(route_count):
        mix_of = mix_of + jnp.where(ids_ref[:, k : k + 1] == expert_of, mix[:, k : k + 1], 0.0)
    repeat = jnp.where(
        iota((experts, block_rows), 1) // ROWS == iota((experts, block_rows), 0), 1.0, 0.0
    ).astype(jnp.bfloat16)
    slot_ref[...] = jnp.dot(slot.astype(jnp.bfloat16), repeat, preferred_element_type=jnp.float32)
    mix_ref[...] = jnp.dot(
        mix_of.astype(jnp.bfloat16), repeat, preferred_element_type=jnp.float32
    )


def plan(expert_ids, gate_weights, experts):
    shape = (expert_ids.shape[0], experts * ROWS)
    return pl.pallas_call(
        plan_kernel,
        out_shape=(pltpu.HBM(shape, jnp.float32), pltpu.HBM(shape, jnp.float32)),
        compiler_params=pltpu.CompilerParams(vmem_limit_bytes=16 * MIB),
        cost_estimate=pl.CostEstimate(flops=10**8, bytes_accessed=10**6, transcendentals=0),
        name="plan",
    )(expert_ids, gate_weights)


def dequant_kernel(place, scale_ref, weight_ref, out_ref):
    row_blocks, col_blocks = (n // QBLK for n in weight_ref.shape)
    step = pl.program_id(0)
    for i in range(row_blocks):
        rows = slice(i * QBLK, (i + 1) * QBLK)
        for j in range(col_blocks):
            scale = scale_ref[step * row_blocks + i, j]
            scaled = weight_ref[rows, j * QBLK : (j + 1) * QBLK].astype(jnp.float32) * scale
            out_ref[rows, place(j) * QBLK : (place(j) + 1) * QBLK] = scaled.astype(out_ref.dtype)


def dequant(weight, scales, rows, place):
    row_count, col_count = weight.shape
    block = pl.BlockSpec((rows, col_count), lambda i: (i, 0))
    return pl.pallas_call(
        functools.partial(dequant_kernel, place),
        grid=(row_count // rows,),
        out_shape=pltpu.HBM(weight.shape, weight.dtype),
        in_specs=[pl.BlockSpec(memory_space=pltpu.SMEM), block],
        out_specs=block,
        compiler_params=pltpu.CompilerParams(vmem_limit_bytes=16 * MIB),
        cost_estimate=pl.CostEstimate(
            flops=row_count * col_count, bytes_accessed=4 * row_count * col_count, transcendentals=0
        ),
        name="dequant",
    )(scales, pltpu.with_memory_space_constraint(weight, pltpu.HBM))


def expert_kernel(
    hidden_tile, given_ref, gu_given_ref, down_given_ref, out_ref,
    in_ref, gu_ref, down_ref, x_ref, hidden_ref, extra_ref, result_ref,
    in_sem, gu_sem, down_sem, out_sem,
):
    step = pl.program_id(0)
    group_width = result_ref.shape[2]
    runs, tiles = in_sem.shape[0], gu_sem.shape[0]
    span = in_ref.shape[0] // runs
    sources = span // ROWS
    kept = sources * SLOTS
    up_end = runs + tiles
    per_tile = ROWS // tiles

    def in_copy(run):
        rows = pl.ds(pl.multiple_of(run * span, span), span)
        return pltpu.make_async_copy(given_ref.at[rows], in_ref.at[rows], in_sem.at[run])

    def gu_copy(tile):
        cols = pl.ds(pl.multiple_of(tile * 2 * hidden_tile, 2 * hidden_tile), 2 * hidden_tile)
        return pltpu.make_async_copy(gu_given_ref.at[:, cols], gu_ref.at[:, cols], gu_sem.at[tile])

    def down_copy(turn):
        cols = pl.ds(pl.multiple_of((turn + SLOTS) % ROWS * group_width, group_width), group_width)
        return pltpu.make_async_copy(
            down_given_ref.at[:, cols], down_ref.at[:, cols], down_sem.at[turn]
        )

    def out_copy(group):
        cols = pl.ds(pl.multiple_of(group * group_width, group_width), group_width)
        return pltpu.make_async_copy(result_ref.at[group], out_ref.at[:, cols], out_sem.at[group])

    @pl.when(step == 0)
    def _():
        for run in range(runs):
            in_copy(run).start()
        gu_copy(0).start()

    @pl.when((step >= runs) & (step < up_end))
    def _():
        tile = step - runs
        gu_copy(tile).wait()

        @pl.when(tile + 1 < tiles)
        def _():
            gu_copy(tile + 1).start()

        for i in range(per_tile):
            down_copy(tile * per_tile + i).start()

    @pl.when(step < runs)
    def _():
        in_copy(step).wait()

    @pl.when(step >= up_end)
    def _():
        down_copy(step - up_end).wait()

    def turned(back):
        to, come = iota((span, span), 1 if back else 0), iota((span, span), 0 if back else 1)
        same = (to // sources == come % ROWS) & (to % sources == come // ROWS)
        return jnp.where(same, 1.0, 0.0).astype(jnp.bfloat16)

    @pl.when(step < runs)
    def _():
        order = turned(False)
        base = pl.multiple_of(step * kept, kept)
        rows = pl.ds(pl.multiple_of(step * span, span), span)
        for group in range(SLOTS):
            moved = jnp.dot(
                order,
                in_ref[rows, group * group_width : (group + 1) * group_width],
                preferred_element_type=jnp.float32,
            ).astype(x_ref.dtype)
            for row in range(ROWS):
                slot, feature = (row, group) if row < SLOTS else (group, row)
                x_ref[
                    pl.ds(base + slot * sources, sources),
                    feature * group_width : (feature + 1) * group_width,
                ] = moved[row * sources : (row + 1) * sources]

    @pl.when((step >= runs) & (step < up_end))
    def _():
        tile = step - runs
        both = pl.ds(pl.multiple_of(tile * 2 * hidden_tile, 2 * hidden_tile), 2 * hidden_tile)
        pre = jnp.dot(x_ref[...], gu_ref[:, both], preferred_element_type=jnp.float32)
        gate, up = pre[:, :hidden_tile], pre[:, hidden_tile:]
        start = pl.multiple_of(tile * hidden_tile, hidden_tile)
        hidden_ref[:, pl.ds(start, hidden_tile)] = (gate / (1.0 + jnp.exp(-gate)) * up).astype(
            hidden_ref.dtype
        )

    def product(feature):
        cols = pl.ds(pl.multiple_of(feature * group_width, group_width), group_width)
        return jnp.dot(
            hidden_ref[...], down_ref[:, cols], preferred_element_type=jnp.float32
        ).astype(jnp.bfloat16)

    @pl.when((step >= up_end) & (step < up_end + EXTRA))
    def _():
        extra_ref[step - up_end] = product(step - up_end + SLOTS)

    @pl.when(step >= up_end + EXTRA)
    def _():
        group = step - (up_end + EXTRA)
        result = product(group)
        order = turned(True)
        for run in range(runs):
            start = pl.multiple_of(run * kept + group * sources, sources)
            gathered = jnp.concatenate(
                [result[run * kept : (run + 1) * kept]]
                + [extra_ref[i, pl.ds(start, sources), :] for i in range(EXTRA)],
                axis=0,
            )
            result_ref[group, run * span : (run + 1) * span, :] = jnp.dot(
                order, gathered, preferred_element_type=jnp.float32
            ).astype(result_ref.dtype)
        out_copy(group).start()

    @pl.when(step == up_end + ROWS - 1)
    def _():
        for group in range(SLOTS):
            out_copy(group).wait()


def expert(arrived, gate_up, down, hidden_tile):
    block_rows, packed_width = arrived.shape
    feat_width, hidden_width = gate_up.shape[0], down.shape[0]
    group_width = feat_width // ROWS
    live_rows = block_rows // ROWS * SLOTS
    runs = block_rows // 256
    tiles = hidden_width // hidden_tile
    given = pl.BlockSpec(memory_space=pl.ANY)

    return pl.pallas_call(
        functools.partial(expert_kernel, hidden_tile),
        grid=(runs + tiles + ROWS,),
        out_shape=pltpu.HBM(arrived.shape, arrived.dtype),
        in_specs=[given, given, given],
        out_specs=given,
        scratch_shapes=[
            pltpu.VMEM(arrived.shape, jnp.bfloat16),
            pltpu.VMEM(gate_up.shape, jnp.bfloat16),
            pltpu.VMEM(down.shape, jnp.bfloat16),
            pltpu.VMEM((live_rows, feat_width), jnp.bfloat16),
            pltpu.VMEM((live_rows, hidden_width), jnp.bfloat16),
            pltpu.VMEM((EXTRA, live_rows, group_width), jnp.bfloat16),
            pltpu.VMEM((SLOTS, block_rows, group_width), jnp.bfloat16),
            pltpu.SemaphoreType.DMA((runs,)),
            pltpu.SemaphoreType.DMA((tiles,)),
            pltpu.SemaphoreType.DMA((ROWS,)),
            pltpu.SemaphoreType.DMA((SLOTS,)),
        ],
        compiler_params=pltpu.CompilerParams(vmem_limit_bytes=56 * MIB),
        cost_estimate=pl.CostEstimate(
            flops=2 * live_rows * 3 * feat_width * hidden_width,
            bytes_accessed=6 * feat_width * hidden_width + 4 * block_rows * packed_width,
            transcendentals=live_rows * hidden_width,
        ),
        name="expert",
    )(*(pltpu.with_memory_space_constraint(a, pltpu.HBM) for a in (arrived, gate_up, down)))


def combine_kernel(
    slot_given_ref, mix_given_ref, given_ref, out_ref,
    slot_ref, mix_ref, in_ref, weight_ref, slot_sem, mix_sem, in_sem,
):
    tok_rows, feat_width = out_ref.shape
    group_width = feat_width // ROWS

    def group(g):
        return slice(g * group_width, (g + 1) * group_width)

    plans = [
        pltpu.make_async_copy(slot_given_ref, slot_ref, slot_sem),
        pltpu.make_async_copy(mix_given_ref, mix_ref, mix_sem),
    ]
    reads = [
        pltpu.make_async_copy(given_ref.at[:, group(g)], in_ref.at[:, group(g)], in_sem.at[g])
        for g in range(SLOTS)
    ]
    for copy in plans + reads:
        copy.start()
    for copy in plans:
        copy.wait()
    slot, mix = slot_ref[...], mix_ref[...]
    row = iota(slot.shape, 1) % ROWS
    own = jnp.where((row < SLOTS) & (slot == row.astype(jnp.float32)), mix, 0.0)
    own = own.astype(weight_ref.dtype)
    for g in range(SLOTS):
        weight_ref[g, :tok_rows] = own
        here = jnp.where(slot == float(g), mix, 0.0)
        for i in range(EXTRA):
            weight_ref[g, (1 + i) * tok_rows : (2 + i) * tok_rows] = jnp.where(
                row == SLOTS + i, here, 0.0
            ).astype(weight_ref.dtype)
    total = jnp.zeros((EXTRA * tok_rows, group_width), jnp.float32)
    for g in range(SLOTS):
        reads[g].wait()
        part = jnp.dot(weight_ref[g], in_ref[:, group(g)], preferred_element_type=jnp.float32)
        out_ref[:, group(g)] = part[:tok_rows].astype(out_ref.dtype)
        total = total + part[tok_rows:]
    for i in range(EXTRA):
        out_ref[:, group(SLOTS + i)] = total[i * tok_rows : (i + 1) * tok_rows].astype(out_ref.dtype)


def combine(planned, returned, out_shape):
    slot, mix = planned
    given = pl.BlockSpec(memory_space=pl.ANY)
    return pl.pallas_call(
        combine_kernel,
        out_shape=out_shape,
        in_specs=[given, given, given],
        out_specs=pl.BlockSpec(memory_space=pltpu.VMEM),
        scratch_shapes=[
            pltpu.VMEM(slot.shape, slot.dtype),
            pltpu.VMEM(mix.shape, mix.dtype),
            pltpu.VMEM(returned.shape, returned.dtype),
            pltpu.VMEM((SLOTS, (1 + EXTRA) * out_shape.shape[0], slot.shape[1]), jnp.bfloat16),
            pltpu.SemaphoreType.DMA,
            pltpu.SemaphoreType.DMA,
            pltpu.SemaphoreType.DMA((SLOTS,)),
        ],
        compiler_params=pltpu.CompilerParams(vmem_limit_bytes=32 * MIB),
        name="combine",
    )(*(pltpu.with_memory_space_constraint(a, pltpu.HBM) for a in (slot, mix, returned)))


def exchange(blocks, experts):
    shape = blocks.shape
    moved = lax.all_to_all(
        blocks.reshape(experts, ROWS, shape[1]),
        ("expert", "helper"),
        split_axis=0,
        concat_axis=0,
        tiled=True,
    )
    return moved.reshape(shape)


def shards(tokens, expert_ids, gate_weights, w_gate_up, gu_scales, w_down, down_scales):
    experts = lax.axis_size("expert") * lax.axis_size("helper")
    hidden_width = w_down.shape[1]
    tile = 256
    arrived = exchange(pack(tokens, expert_ids, experts), experts)
    wide = tile // QBLK

    def place(j):
        part, block = divmod(j, hidden_width // QBLK)
        return block // wide * 2 * wide + part * wide + block % wide

    gate_up = dequant(w_gate_up[0], gu_scales[0], 256, place)
    down = dequant(w_down[0], down_scales[0], 128, lambda j: j)
    planned = plan(expert_ids, gate_weights, experts)
    returned = exchange(expert(arrived, gate_up, down, tile), experts)
    return combine(planned, returned, jax.ShapeDtypeStruct(tokens.shape, tokens.dtype))


def solution(mesh):
    rows = ("expert", "helper")
    placed = (P(rows, None),) * 3 + (P(rows, None, None),) * 4
    return jax.shard_map(
        shards, mesh=mesh, in_specs=placed, out_specs=P(rows, None), check_vma=False
    )
```

time: 192 us -> 182 us (0.948)
  local copies, waits for them, and re-layouts: 21.5 us -> 0.95 us
  waiting for transfers between devices: 84.4 us -> 98 us
  Pallas kernels: 67.4 us -> 64.5 us
    unnamed x23 -> x13, local copies, waits for them, and re-layouts: 21.5 us -> 0.95 us
    all_to_all x2, waiting for transfers between devices: 84.4 us -> 98 us  [exchange(): lax.all_to_all(blocks.reshape(experts, ROWS, shape[1]), ('expert', 'helpe...]
    pallas_call x6, Pallas kernels: 67.4 us -> 64.5 us  [the longest x2 28.6 us: dequant(): pl.pallas_call(functools.partial(dequant_kernel, place), grid=(row_count...]
  transfers between devices with their start and end apart: 2 -> 2, of which waited for: 2 -> 2; matrix products, arithmetic and copies ran while one was open for 0% -> 0% of each run, Pallas kernels for 15% -> 17%
where the time goes in v1:
time: 182 us; the launch traced here: 181 us
  waiting for transfers between devices  98 us (54%)
  Pallas kernels  64.5 us (35%)
  starting transfers between devices  17.5 us (10%)
    all_to_all x2, waiting for transfers between devices, exchange(): lax.all_to_all(blocks.reshape(experts, ROWS, shape[1]), ('expert', 'helpe...  98 us
    pallas_call x2, Pallas kernels, dequant(): pl.pallas_call(functools.partial(dequant_kernel, place), grid=(row_count...  28.6 us
    pallas_call x1, Pallas kernels, expert(): pl.pallas_call(functools.partial(expert_kernel, hidden_tile), grid=(runs...  25.3 us
    all_to_all x2, starting transfers between devices, exchange(): lax.all_to_all(blocks.reshape(experts, ROWS, shape[1]), ('expert', 'helpe...  17.5 us
    pallas_call x1, Pallas kernels, combine(): pl.pallas_call(combine_kernel, out_shape=out_shape, in_specs=[given, give...  5.38 us
    pallas_call x1, Pallas kernels, pack(): pl.pallas_call(pack_kernel, out_shape=pltpu.HBM(shape, tokens.dtype), in_...  3.9 us
  transfers between devices with their start and end apart: 2, of which 2 were waited for; matrix products, arithmetic and copies ran while one was open for 0% of the time, Pallas kernels for 17%

profile of v1, /device:TPU:1, one launch (start us, length us, event | category | flops | bytes accessed | tf_op | source)
XLA Modules:
  0.0 181.0 jit_solution(10789955844515350725)
XLA Ops:
  0.0 0.0 copy-start
  0.0 0.7 copy-done
  0.7 0.0 copy-start.3
  0.7 0.0 copy-start.2
  0.7 3.9 %pack.1 = bf16[1024,2560]{1,0:T(8,128)(2,1)} custom-call(s32[8,64]{1,0:T(8,128)S(1)} %bitcast.10, bf16[64,4096]{1,0:T(8,128)(2,1)} %given_ref.1), custom_call_target="tpu_custom_call" | custom-call | tf_op jit(solution)/shard_map/pack/pallas_call | solution.py:98
  4.6 11.9 %all-to-all-start = ((bf16[128,8,2560]{2,1,0:T(8,128)(2,1)}), bf16[128,8,2560]{2,1,0:T(8,128)(2,1)}, u32[]{:S(2)}, u32[]{:S(2)}) async-start(bf16[128,8,2560]{2,1,0:T(8,128)(2,1)} %bitcast.12), calls=%async_computation | async-start | bytes 10485760 | tf_op jit(solution)/shard_map/all_to_all | solution.py:404
  16.5 0.0 copy-done.3
  16.5 0.1 copy.10
  16.6 0.0 copy-done.2
  16.6 9.7 %dequant.3.down_given_ref = bf16[1024,4096]{1,0:T(8,128)(2,1)} custom-call(f32[8,32]{1,0:T(8,128)S(1)} %bitcast.11, bf16[1024,4096]{1,0:T(8,128)(2,1)} %bitcast.14), custom_call_target="tpu_custom_call" | custom-call | flops 4194304 | bytes 16777216 | tf_op jit(solution)/shard_map/dequant/pallas_call | solution.py:160
  26.3 18.9 %dequant.2.gu_given_ref = bf16[4096,2048]{1,0:T(8,128)(2,1)} custom-call(f32[32,16]{1,0:T(8,128)S(1)} %bitcast.9, bf16[4096,2048]{1,0:T(8,128)(2,1)} %bitcast.13), custom_call_target="tpu_custom_call" | custom-call | flops 8388608 | bytes 33554432 | tf_op jit(solution)/shard_map/dequant/pallas_call | solution.py:160
  45.2 35.4 %all-to-all-done = bf16[128,8,2560]{2,1,0:T(8,128)(2,1)} async-done(((bf16[128,8,2560]{2,1,0:T(8,128)(2,1)}), bf16[128,8,2560]{2,1,0:T(8,128)(2,1)}, u32[]{:S(2)}, u32[]{:S(2)}) %all-to-all-start) | async-done | bytes 5242912 | tf_op jit(solution)/shard_map/all_to_all | solution.py:404
  80.6 25.3 %expert.1 = bf16[1024,2560]{1,0:T(8,128)(2,1)} custom-call(bf16[1024,2560]{1,0:T(8,128)(2,1)} %bitcast.2.given_ref, bf16[4096,2048]{1,0:T(8,128)(2,1)} %dequant.2.gu_given_ref, bf16[1024,4096]{1,0:T(8,128)(2,1)} %dequant.3.down_given_ref), custom_call_target="tpu_custom_call" | custom-call | flops 16106127360 | bytes 35651584 | tf_op jit(solution)/shard_map/expert/pallas_call | solution.py:308
  105.9 0.0 copy-start.1
  105.9 0.0 copy-start.4
  105.9 5.6 %all-to-all-start.1 = ((bf16[128,8,2560]{2,1,0:T(8,128)(2,1)}), bf16[128,8,2560]{2,1,0:T(8,128)(2,1)}, u32[]{:S(2)}, u32[]{:S(2)}) async-start(bf16[128,8,2560]{2,1,0:T(8,128)(2,1)} %bitcast.15), calls=%async_computation.1 | async-start | bytes 10485760 | tf_op jit(solution)/shard_map/all_to_all | solution.py:404
  111.5 0.0 copy-done.1
  111.5 0.1 copy.8.ids_ref
  111.6 0.0 copy-done.4
  111.6 0.1 copy.9.gate_ref
  111.7 1.3 plan.1
  113.0 62.6 %all-to-all-done.1 = bf16[128,8,2560]{2,1,0:T(8,128)(2,1)} async-done(((bf16[128,8,2560]{2,1,0:T(8,128)(2,1)}), bf16[128,8,2560]{2,1,0:T(8,128)(2,1)}, u32[]{:S(2)}, u32[]{:S(2)}) %all-to-all-start.1) | async-done | bytes 5242912 | tf_op jit(solution)/shard_map/all_to_all | solution.py:404
  175.6 5.4 %combine.1 = bf16[64,4096]{1,0:T(8,128)(2,1)} custom-call(f32[64,1024]{1,0:T(8,128)} %get-tuple-element.7.slot_given_ref, f32[64,1024]{1,0:T(8,128)} %get-tuple-element.8.mix_given_ref, bf16[1024,2560]{1,0:T(8,128)(2,1)} %bitcast.8.given_ref), custom_call_target="tpu_custom_call" | custom-call | tf_op jit(solution)/shard_map/combine/pallas_call | solution.py:383
Async XLA Ops:
  0.0 0.7 copy-start
  0.7 15.8 %copy-start.3 = (f32[1,32,16]{1,2,0:T(8,128)S(1)}, f32[1,32,16]{1,2,0:T(8,128)}, u32[]{:S(2)}) copy-start(f32[1,32,16]{1,2,0:T(8,128)} %param.11) | copy-start | bytes 6148
  0.7 15.9 %copy-start.2 = (f32[1,8,32]{2,1,0:T(8,128)S(1)}, f32[1,8,32]{2,1,0:T(8,128)}, u32[]{:S(2)}) copy-start(f32[1,8,32]{2,1,0:T(8,128)} %param.13) | copy-start | bytes 3076
  4.6 76.0 %all-to-all-start = ((bf16[128,8,2560]{2,1,0:T(8,128)(2,1)}), bf16[128,8,2560]{2,1,0:T(8,128)(2,1)}, u32[]{:S(2)}, u32[]{:S(2)}) async-start(bf16[128,8,2560]{2,1,0:T(8,128)(2,1)} %bitcast.12), calls=%async_computation | async-start | bytes 10485760 | tf_op jit(solution)/shard_map/all_to_all | solution.py:404
  105.9 5.6 %copy-start.1 = (s32[64,8]{0,1:T(8,128)S(1)}, s32[64,8]{0,1:T(8,128)}, u32[]{:S(2)}) copy-start(s32[64,8]{0,1:T(8,128)} %param.8) | copy-start | bytes 6148
  105.9 5.7 %copy-start.4 = (f32[64,8]{0,1:T(8,128)S(1)}, f32[64,8]{0,1:T(8,128)}, u32[]{:S(2)}) copy-start(f32[64,8]{0,1:T(8,128)} %param.9) | copy-start | bytes 6148
  105.9 69.7 %all-to-all-start.1 = ((bf16[128,8,2560]{2,1,0:T(8,128)(2,1)}), bf16[128,8,2560]{2,1,0:T(8,128)(2,1)}, u32[]{:S(2)}, u32[]{:S(2)}) async-start(bf16[128,8,2560]{2,1,0:T(8,128)(2,1)} %bitcast.15), calls=%async_computation.1 | async-start | bytes 10485760 | tf_op jit(solution)/shard_map/all_to_all | solution.py:404

commit v2 on v1

--- a/solution.py
+++ b/solution.py
@@ -45,16 +45,22 @@
 
 
 ALWAYS = 99.0
-
-
-def pack_kernel(ids_ref, given_ref, out_ref, tok_ref, block_ref, slot_ref, tok_sem, out_sem):
+AHEAD = 3
+
+
+def pack_kernel(
+    ids_given_ref, given_ref, out_ref, ids_ref, tok_ref, block_ref, slot_ref, ids_sem, tok_sem, out_sem
+):
     tok_rows, feat_width = tok_ref.shape
     group_width = feat_width // ROWS
     block_rows = block_ref.shape[0]
     experts = block_rows // ROWS
     parts = 1 + EXTRA
+    fetch_ids = pltpu.make_async_copy(ids_given_ref, ids_ref, ids_sem)
+    fetch_ids.start()
     fetch = pltpu.make_async_copy(given_ref, tok_ref, tok_sem)
     fetch.start()
+    fetch_ids.wait()
 
     slot = slots_for(ids_ref[...], experts).astype(jnp.bfloat16)
     repeat = jnp.where(
@@ -98,18 +104,20 @@
     return pl.pallas_call(
         pack_kernel,
         out_shape=pltpu.HBM(shape, tokens.dtype),
-        in_specs=[pl.BlockSpec(memory_space=pltpu.VMEM), pl.BlockSpec(memory_space=pl.ANY)],
+        in_specs=[pl.BlockSpec(memory_space=pl.ANY)] * 2,
         out_specs=pl.BlockSpec(memory_space=pl.ANY),
         scratch_shapes=[
+            pltpu.VMEM(expert_ids.shape[::-1], expert_ids.dtype),
             pltpu.VMEM(tokens.shape, tokens.dtype),
             pltpu.VMEM(shape, tokens.dtype),
             pltpu.VMEM((shape[0], (1 + EXTRA) * tok_rows), jnp.float32),
+            pltpu.SemaphoreType.DMA,
             pltpu.SemaphoreType.DMA,
             pltpu.SemaphoreType.DMA((SLOTS,)),
         ],
         compiler_params=pltpu.CompilerParams(vmem_limit_bytes=32 * MIB),
         name="pack",
-    )(expert_ids.T, pltpu.with_memory_space_constraint(tokens, pltpu.HBM))
+    )(*(pltpu.with_memory_space_constraint(a, pltpu.HBM) for a in (expert_ids.T, tokens)))
 
 
 def plan_kernel(ids_ref, gate_ref, slot_ref, mix_ref):
@@ -173,127 +181,98 @@
 
 def expert_kernel(
     hidden_tile, given_ref, gu_given_ref, down_given_ref, out_ref,
-    in_ref, gu_ref, down_ref, x_ref, hidden_ref, extra_ref, result_ref,
-    in_sem, gu_sem, down_sem, out_sem,
+    in_ref, gu_ref, down_ref, x_ref, hidden_ref, result_ref, in_sem, gu_sem, down_sem, out_sem,
 ):
-    step = pl.program_id(0)
     group_width = result_ref.shape[2]
     runs, tiles = in_sem.shape[0], gu_sem.shape[0]
     span = in_ref.shape[0] // runs
     sources = span // ROWS
     kept = sources * SLOTS
-    up_end = runs + tiles
-    per_tile = ROWS // tiles
-
-    def in_copy(run):
-        rows = pl.ds(pl.multiple_of(run * span, span), span)
-        return pltpu.make_async_copy(given_ref.at[rows], in_ref.at[rows], in_sem.at[run])
-
-    def gu_copy(tile):
-        cols = pl.ds(pl.multiple_of(tile * 2 * hidden_tile, 2 * hidden_tile), 2 * hidden_tile)
-        return pltpu.make_async_copy(gu_given_ref.at[:, cols], gu_ref.at[:, cols], gu_sem.at[tile])
-
-    def down_copy(turn):
-        cols = pl.ds(pl.multiple_of((turn + SLOTS) % ROWS * group_width, group_width), group_width)
-        return pltpu.make_async_copy(
-            down_given_ref.at[:, cols], down_ref.at[:, cols], down_sem.at[turn]
-        )
-
-    def out_copy(group):
-        cols = pl.ds(pl.multiple_of(group * group_width, group_width), group_width)
-        return pltpu.make_async_copy(result_ref.at[group], out_ref.at[:, cols], out_sem.at[group])
-
-    @pl.when(step == 0)
-    def _():
-        for run in range(runs):
-            in_copy(run).start()
-        gu_copy(0).start()
-
-    @pl.when((step >= runs) & (step < up_end))
-    def _():
-        tile = step - runs
-        gu_copy(tile).wait()
-
-        @pl.when(tile + 1 < tiles)
-        def _():
-            gu_copy(tile + 1).start()
-
-        for i in range(per_tile):
-            down_copy(tile * per_tile + i).start()
-
-    @pl.when(step < runs)
-    def _():
-        in_copy(step).wait()
-
-    @pl.when(step >= up_end)
-    def _():
-        down_copy(step - up_end).wait()
+    order = (*range(SLOTS - 1, ROWS), *range(SLOTS - 1))
+
+    def group(g):
+        return slice(g * group_width, (g + 1) * group_width)
+
+    def run_rows(run, rows):
+        return slice(run * rows, (run + 1) * rows)
+
+    def copies(given, held, sem, places):
+        return [
+            pltpu.make_async_copy(given.at[p], held.at[p], sem.at[i]) for i, p in enumerate(places)
+        ]
+
+    in_copies = copies(given_ref, in_ref, in_sem, [(run_rows(r, span),) for r in range(runs)])
+    gu_places = [(slice(None), run_rows(t, 2 * hidden_tile)) for t in range(tiles)]
+    gu_copies = copies(gu_given_ref, gu_ref, gu_sem, gu_places)
+    down_copies = copies(down_given_ref, down_ref, down_sem, [(slice(None), group(f)) for f in order])
+    out_copies = [
+        pltpu.make_async_copy(result_ref.at[g], out_ref.at[:, group(g)], out_sem.at[g])
+        for g in range(SLOTS)
+    ]
 
     def turned(back):
         to, come = iota((span, span), 1 if back else 0), iota((span, span), 0 if back else 1)
         same = (to // sources == come % ROWS) & (to % sources == come // ROWS)
         return jnp.where(same, 1.0, 0.0).astype(jnp.bfloat16)
 
-    @pl.when(step < runs)
-    def _():
-        order = turned(False)
-        base = pl.multiple_of(step * kept, kept)
-        rows = pl.ds(pl.multiple_of(step * span, span), span)
-        for group in range(SLOTS):
+    for copy in in_copies + gu_copies[:1]:
+        copy.start()
+    unpack = turned(False)
+    for run in range(runs):
+        in_copies[run].wait()
+        for g in range(SLOTS):
             moved = jnp.dot(
-                order,
-                in_ref[rows, group * group_width : (group + 1) * group_width],
-                preferred_element_type=jnp.float32,
+                unpack, in_ref[run_rows(run, span), group(g)], preferred_element_type=jnp.float32
             ).astype(x_ref.dtype)
             for row in range(ROWS):
-                slot, feature = (row, group) if row < SLOTS else (group, row)
-                x_ref[
-                    pl.ds(base + slot * sources, sources),
-                    feature * group_width : (feature + 1) * group_width,
-                ] = moved[row * sources : (row + 1) * sources]
-
-    @pl.when((step >= runs) & (step < up_end))
-    def _():
-        tile = step - runs
-        both = pl.ds(pl.multiple_of(tile * 2 * hidden_tile, 2 * hidden_tile), 2 * hidden_tile)
-        pre = jnp.dot(x_ref[...], gu_ref[:, both], preferred_element_type=jnp.float32)
+                slot, feature = (row, g) if row < SLOTS else (g, row)
+                first = run * kept + slot * sources
+                x_ref[first : first + sources, group(feature)] = moved[run_rows(row, sources)]
+    for tile in range(tiles):
+        gu_copies[tile].wait()
+        for copy in gu_copies[tile + 1 : tile + 2] + down_copies[
+            tile * ROWS // tiles : (tile + 1) * ROWS // tiles
+        ]:
+            copy.start()
+        pre = jnp.dot(x_ref[...], gu_ref[gu_places[tile]], preferred_element_type=jnp.float32)
         gate, up = pre[:, :hidden_tile], pre[:, hidden_tile:]
-        start = pl.multiple_of(tile * hidden_tile, hidden_tile)
-        hidden_ref[:, pl.ds(start, hidden_tile)] = (gate / (1.0 + jnp.exp(-gate)) * up).astype(
+        hidden_ref[:, run_rows(tile, hidden_tile)] = (gate / (1.0 + jnp.exp(-gate)) * up).astype(
             hidden_ref.dtype
         )
-
-    def product(feature):
-        cols = pl.ds(pl.multiple_of(feature * group_width, group_width), group_width)
+    pack_again = turned(True)
+
+    def product(first, count):
+        cols = slice(first * group_width, (first + count) * group_width)
         return jnp.dot(
             hidden_ref[...], down_ref[:, cols], preferred_element_type=jnp.float32
-        ).astype(jnp.bfloat16)
-
-    @pl.when((step >= up_end) & (step < up_end + EXTRA))
-    def _():
-        extra_ref[step - up_end] = product(step - up_end + SLOTS)
-
-    @pl.when(step >= up_end + EXTRA)
-    def _():
-        group = step - (up_end + EXTRA)
-        result = product(group)
-        order = turned(True)
+        ).astype(x_ref.dtype)
+
+    def give(feature, result):
         for run in range(runs):
-            start = pl.multiple_of(run * kept + group * sources, sources)
+            first = run * kept + feature * sources
             gathered = jnp.concatenate(
-                [result[run * kept : (run + 1) * kept]]
-                + [extra_ref[i, pl.ds(start, sources), :] for i in range(EXTRA)],
+                [result[run_rows(run, kept)]]
+                + [x_ref[first : first + sources, group(f)] for f in range(SLOTS, ROWS)],
                 axis=0,
             )
-            result_ref[group, run * span : (run + 1) * span, :] = jnp.dot(
-                order, gathered, preferred_element_type=jnp.float32
+            result_ref[feature, run_rows(run, span), :] = jnp.dot(
+                pack_again, gathered, preferred_element_type=jnp.float32
             ).astype(result_ref.dtype)
-        out_copy(group).start()
-
-    @pl.when(step == up_end + ROWS - 1)
-    def _():
-        for group in range(SLOTS):
-            out_copy(group).wait()
+        out_copies[feature].start()
+
+    for copy in down_copies[:EXTRA + 1]:
+        copy.wait()
+    result = product(SLOTS - 1, EXTRA + 1)
+    x_ref[:, SLOTS * group_width :] = result[:, group_width:]
+    give(SLOTS - 1, result[:, :group_width])
+    for copy in down_copies[EXTRA + 1 :]:
+        copy.wait()
+    for feature in range(0, SLOTS - 1, 2):
+        result = product(feature, 2)
+        give(feature, result[:, :group_width])
+        give(feature + 1, result[:, group_width:])
+    for copy in out_copies:
+        copy.wait()
 
 
 def expert(arrived, gate_up, down, hidden_tile):
@@ -307,7 +286,6 @@
 
     return pl.pallas_call(
         functools.partial(expert_kernel, hidden_tile),
-        grid=(runs + tiles + ROWS,),
         out_shape=pltpu.HBM(arrived.shape, arrived.dtype),
         in_specs=[given, given, given],
         out_specs=given,
@@ -317,7 +295,6 @@
             pltpu.VMEM(down.shape, jnp.bfloat16),
             pltpu.VMEM((live_rows, feat_width), jnp.bfloat16),
             pltpu.VMEM((live_rows, hidden_width), jnp.bfloat16),
-            pltpu.VMEM((EXTRA, live_rows, group_width), jnp.bfloat16),
             pltpu.VMEM((SLOTS, block_rows, group_width), jnp.bfloat16),
             pltpu.SemaphoreType.DMA((runs,)),
             pltpu.SemaphoreType.DMA((tiles,)),
@@ -352,7 +329,7 @@
         pltpu.make_async_copy(given_ref.at[:, group(g)], in_ref.at[:, group(g)], in_sem.at[g])
         for g in range(SLOTS)
     ]
-    for copy in plans + reads:
+    for copy in plans + reads[:AHEAD]:
         copy.start()
     for copy in plans:
         copy.wait()
@@ -370,6 +347,8 @@
     total = jnp.zeros((EXTRA * tok_rows, group_width), jnp.float32)
     for g in range(SLOTS):
         reads[g].wait()
+        for copy in reads[g + AHEAD : g + AHEAD + 1]:
+            copy.start()
         part = jnp.dot(weight_ref[g], in_ref[:, group(g)], preferred_element_type=jnp.float32)
         out_ref[:, group(g)] = part[:tok_rows].astype(out_ref.dtype)
         total = total + part[tok_rows:]

time: 182 us -> 180 us (0.989)
  no operation moved by 1% of the time
where the time goes in v2:
time: 180 us; the launch traced here: 179 us
  waiting for transfers between devices  98 us (54%)
  Pallas kernels  63 us (35%)
  starting transfers between devices  17.5 us (10%)
    all_to_all x2, waiting for transfers between devices, exchange(): lax.all_to_all(blocks.reshape(experts, ROWS, shape[1]), ('expert', 'helpe...  98 us
    pallas_call x2, Pallas kernels, dequant(): pl.pallas_call(functools.partial(dequant_kernel, place), grid=(row_count...  28.6 us
    pallas_call x1, Pallas kernels, expert(): pl.pallas_call(functools.partial(expert_kernel, hidden_tile), out_shape=p...  24 us
    all_to_all x2, starting transfers between devices, exchange(): lax.all_to_all(blocks.reshape(experts, ROWS, shape[1]), ('expert', 'helpe...  17.5 us
    pallas_call x1, Pallas kernels, combine(): pl.pallas_call(combine_kernel, out_shape=out_shape, in_specs=[given, give...  4.89 us
    pallas_call x1, Pallas kernels, pack(): pl.pallas_call(pack_kernel, out_shape=pltpu.HBM(shape, tokens.dtype), in_...  4.17 us
  transfers between devices with their start and end apart: 2, of which 2 were waited for; matrix products, arithmetic and copies ran while one was open for 0% of the time, Pallas kernels for 17%

profile of v2, /device:TPU:1, one launch (start us, length us, event | category | flops | bytes accessed | tf_op | source)
XLA Modules:
  0.0 179.0 jit_solution(8271663891073201267)
XLA Ops:
  0.0 0.0 copy-start.2
  0.0 0.0 copy-start
  0.0 4.2 %pack.1 = bf16[1024,2560]{1,0:T(8,128)(2,1)} custom-call(s32[8,64]{1,0:T(8,128)} %bitcast.15, bf16[64,4096]{1,0:T(8,128)(2,1)} %given_ref.1), custom_call_target="tpu_custom_call" | custom-call | tf_op jit(solution)/shard_map/pack/pallas_call | solution.py:104
  4.2 11.9 %all-to-all-start = ((bf16[128,8,2560]{2,1,0:T(8,128)(2,1)}), bf16[128,8,2560]{2,1,0:T(8,128)(2,1)}, u32[]{:S(2)}, u32[]{:S(2)}) async-start(bf16[128,8,2560]{2,1,0:T(8,128)(2,1)} %bitcast.11), calls=%async_computation | async-start | bytes 10485760 | tf_op jit(solution)/shard_map/all_to_all | solution.py:383
  16.1 0.0 copy-done.2
  16.1 0.1 copy.10
  16.2 0.0 copy-done
  16.2 9.7 %dequant.3.down_given_ref = bf16[1024,4096]{1,0:T(8,128)(2,1)} custom-call(f32[8,32]{1,0:T(8,128)S(1)} %bitcast.10, bf16[1024,4096]{1,0:T(8,128)(2,1)} %bitcast.13), custom_call_target="tpu_custom_call" | custom-call | flops 4194304 | bytes 16777216 | tf_op jit(solution)/shard_map/dequant/pallas_call | solution.py:168
  25.9 18.9 %dequant.2.gu_given_ref = bf16[4096,2048]{1,0:T(8,128)(2,1)} custom-call(f32[32,16]{1,0:T(8,128)S(1)} %bitcast.9, bf16[4096,2048]{1,0:T(8,128)(2,1)} %bitcast.12), custom_call_target="tpu_custom_call" | custom-call | flops 8388608 | bytes 33554432 | tf_op jit(solution)/shard_map/dequant/pallas_call | solution.py:168
  44.8 35.4 %all-to-all-done = bf16[128,8,2560]{2,1,0:T(8,128)(2,1)} async-done(((bf16[128,8,2560]{2,1,0:T(8,128)(2,1)}), bf16[128,8,2560]{2,1,0:T(8,128)(2,1)}, u32[]{:S(2)}, u32[]{:S(2)}) %all-to-all-start) | async-done | bytes 5242912 | tf_op jit(solution)/shard_map/all_to_all | solution.py:383
  80.2 24.0 %expert.1 = bf16[1024,2560]{1,0:T(8,128)(2,1)} custom-call(bf16[1024,2560]{1,0:T(8,128)(2,1)} %bitcast.2.given_ref, bf16[4096,2048]{1,0:T(8,128)(2,1)} %dequant.2.gu_given_ref, bf16[1024,4096]{1,0:T(8,128)(2,1)} %dequant.3.down_given_ref), custom_call_target="tpu_custom_call" | custom-call | flops 16106127360 | bytes 35651584 | tf_op jit(solution)/shard_map/expert/pallas_call | solution.py:287
  104.2 0.0 copy-start.1
  104.2 0.0 copy-start.3
  104.2 5.5 %all-to-all-start.1 = ((bf16[128,8,2560]{2,1,0:T(8,128)(2,1)}), bf16[128,8,2560]{2,1,0:T(8,128)(2,1)}, u32[]{:S(2)}, u32[]{:S(2)}) async-start(bf16[128,8,2560]{2,1,0:T(8,128)(2,1)} %bitcast.14), calls=%async_computation.1 | async-start | bytes 10485760 | tf_op jit(solution)/shard_map/all_to_all | solution.py:383
  109.8 0.0 copy-done.1
  109.8 0.1 copy.8.ids_ref
  109.9 0.0 copy-done.3
  109.9 0.1 copy.9.gate_ref
  110.0 1.3 plan.1
  111.3 62.6 %all-to-all-done.1 = bf16[128,8,2560]{2,1,0:T(8,128)(2,1)} async-done(((bf16[128,8,2560]{2,1,0:T(8,128)(2,1)}), bf16[128,8,2560]{2,1,0:T(8,128)(2,1)}, u32[]{:S(2)}, u32[]{:S(2)}) %all-to-all-start.1) | async-done | bytes 5242912 | tf_op jit(solution)/shard_map/all_to_all | solution.py:383
  173.9 4.9 %combine.1 = bf16[64,4096]{1,0:T(8,128)(2,1)} custom-call(f32[64,1024]{1,0:T(8,128)} %get-tuple-element.7.slot_given_ref, f32[64,1024]{1,0:T(8,128)} %get-tuple-element.8.mix_given_ref, bf16[1024,2560]{1,0:T(8,128)(2,1)} %bitcast.8.given_ref), custom_call_target="tpu_custom_call" | custom-call | tf_op jit(solution)/shard_map/combine/pallas_call | solution.py:362
Async XLA Ops:
  0.0 16.1 %copy-start.2 = (f32[1,32,16]{1,2,0:T(8,128)S(1)}, f32[1,32,16]{1,2,0:T(8,128)}, u32[]{:S(2)}) copy-start(f32[1,32,16]{1,2,0:T(8,128)} %param.11) | copy-start | bytes 6148
  0.0 16.2 %copy-start = (f32[1,8,32]{2,1,0:T(8,128)S(1)}, f32[1,8,32]{2,1,0:T(8,128)}, u32[]{:S(2)}) copy-start(f32[1,8,32]{2,1,0:T(8,128)} %param.13) | copy-start | bytes 3076
  4.2 76.0 %all-to-all-start = ((bf16[128,8,2560]{2,1,0:T(8,128)(2,1)}), bf16[128,8,2560]{2,1,0:T(8,128)(2,1)}, u32[]{:S(2)}, u32[]{:S(2)}) async-start(bf16[128,8,2560]{2,1,0:T(8,128)(2,1)} %bitcast.11), calls=%async_computation | async-start | bytes 10485760 | tf_op jit(solution)/shard_map/all_to_all | solution.py:383
  104.2 5.6 %copy-start.1 = (s32[64,8]{0,1:T(8,128)S(1)}, s32[64,8]{0,1:T(8,128)}, u32[]{:S(2)}) copy-start(s32[64,8]{0,1:T(8,128)} %param.8) | copy-start | bytes 6148
  104.2 5.7 %copy-start.3 = (f32[64,8]{0,1:T(8,128)S(1)}, f32[64,8]{0,1:T(8,128)}, u32[]{:S(2)}) copy-start(f32[64,8]{0,1:T(8,128)} %param.9) | copy-start | bytes 6148
  104.2 69.7 %all-to-all-start.1 = ((bf16[128,8,2560]{2,1,0:T(8,128)(2,1)}), bf16[128,8,2560]{2,1,0:T(8,128)(2,1)}, u32[]{:S(2)}, u32[]{:S(2)}) async-start(bf16[128,8,2560]{2,1,0:T(8,128)(2,1)} %bitcast.14), calls=%async_computation.1 | async-start | bytes 10485760 | tf_op jit(solution)/shard_map/all_to_all | solution.py:383

commit v3 on v2

--- a/solution.py
+++ b/solution.py
@@ -45,7 +45,6 @@
 
 
 ALWAYS = 99.0
-AHEAD = 3
 
 
 def pack_kernel(
@@ -120,9 +119,9 @@
     )(*(pltpu.with_memory_space_constraint(a, pltpu.HBM) for a in (expert_ids.T, tokens)))
 
 
-def plan_kernel(ids_ref, gate_ref, slot_ref, mix_ref):
+def plan_kernel(ids_ref, gate_ref, weight_ref):
     tok_rows, route_count = ids_ref.shape
-    block_rows = slot_ref.shape[1]
+    block_rows = weight_ref.shape[2]
     experts = block_rows // ROWS
     gates = gate_ref[...]
     mix = gates / jnp.sum(gates, axis=1, keepdims=True)
@@ -134,17 +133,25 @@
     repeat = jnp.where(
         iota((experts, block_rows), 1) // ROWS == iota((experts, block_rows), 0), 1.0, 0.0
     ).astype(jnp.bfloat16)
-    slot_ref[...] = jnp.dot(slot.astype(jnp.bfloat16), repeat, preferred_element_type=jnp.float32)
-    mix_ref[...] = jnp.dot(
-        mix_of.astype(jnp.bfloat16), repeat, preferred_element_type=jnp.float32
-    )
+    slot = jnp.dot(slot.astype(jnp.bfloat16), repeat, preferred_element_type=jnp.float32)
+    mix = jnp.dot(mix_of.astype(jnp.bfloat16), repeat, preferred_element_type=jnp.float32)
+    row = iota(slot.shape, 1) % ROWS
+    own = jnp.where((row < SLOTS) & (slot == row.astype(jnp.float32)), mix, 0.0)
+    own = own.astype(weight_ref.dtype)
+    for g in range(SLOTS):
+        weight_ref[g, :tok_rows] = own
+        here = jnp.where(slot == float(g), mix, 0.0)
+        for i in range(EXTRA):
+            weight_ref[g, (1 + i) * tok_rows : (2 + i) * tok_rows] = jnp.where(
+                row == SLOTS + i, here, 0.0
+            ).astype(weight_ref.dtype)
 
 
 def plan(expert_ids, gate_weights, experts):
-    shape = (expert_ids.shape[0], experts * ROWS)
+    shape = (SLOTS, (1 + EXTRA) * expert_ids.shape[0], experts * ROWS)
     return pl.pallas_call(
         plan_kernel,
-        out_shape=(pltpu.HBM(shape, jnp.float32), pltpu.HBM(shape, jnp.float32)),
+        out_shape=pltpu.HBM(shape, jnp.bfloat16),
         compiler_params=pltpu.CompilerParams(vmem_limit_bytes=16 * MIB),
         cost_estimate=pl.CostEstimate(flops=10**8, bytes_accessed=10**6, transcendentals=0),
         name="plan",
@@ -181,9 +188,9 @@
 
 def expert_kernel(
     hidden_tile, given_ref, gu_given_ref, down_given_ref, out_ref,
-    in_ref, gu_ref, down_ref, x_ref, hidden_ref, result_ref, in_sem, gu_sem, down_sem, out_sem,
+    in_ref, gu_ref, down_ref, x_ref, hidden_ref, in_sem, gu_sem, down_sem,
 ):
-    group_width = result_ref.shape[2]
+    group_width = x_ref.shape[1] // ROWS
     runs, tiles = in_sem.shape[0], gu_sem.shape[0]
     span = in_ref.shape[0] // runs
     sources = span // ROWS
@@ -205,10 +212,6 @@
     gu_places = [(slice(None), run_rows(t, 2 * hidden_tile)) for t in range(tiles)]
     gu_copies = copies(gu_given_ref, gu_ref, gu_sem, gu_places)
     down_copies = copies(down_given_ref, down_ref, down_sem, [(slice(None), group(f)) for f in order])
-    out_copies = [
-        pltpu.make_async_copy(result_ref.at[g], out_ref.at[:, group(g)], out_sem.at[g])
-        for g in range(SLOTS)
-    ]
 
     def turned(back):
         to, come = iota((span, span), 1 if back else 0), iota((span, span), 0 if back else 1)
@@ -255,10 +258,9 @@
                 + [x_ref[first : first + sources, group(f)] for f in range(SLOTS, ROWS)],
                 axis=0,
             )
-            result_ref[feature, run_rows(run, span), :] = jnp.dot(
+            out_ref[run_rows(run, span), group(feature)] = jnp.dot(
                 pack_again, gathered, preferred_element_type=jnp.float32
-            ).astype(result_ref.dtype)
-        out_copies[feature].start()
+            ).astype(out_ref.dtype)
 
     for copy in down_copies[:EXTRA + 1]:
         copy.wait()
@@ -271,14 +273,11 @@
         result = product(feature, 2)
         give(feature, result[:, :group_width])
         give(feature + 1, result[:, group_width:])
-    for copy in out_copies:
-        copy.wait()
 
 
 def expert(arrived, gate_up, down, hidden_tile):
     block_rows, packed_width = arrived.shape
     feat_width, hidden_width = gate_up.shape[0], down.shape[0]
-    group_width = feat_width // ROWS
     live_rows = block_rows // ROWS * SLOTS
     runs = block_rows // 256
     tiles = hidden_width // hidden_tile
@@ -286,22 +285,20 @@
 
     return pl.pallas_call(
         functools.partial(expert_kernel, hidden_tile),
-        out_shape=pltpu.HBM(arrived.shape, arrived.dtype),
+        out_shape=pltpu.VMEM(arrived.shape, arrived.dtype),
         in_specs=[given, given, given],
-        out_specs=given,
+        out_specs=pl.BlockSpec(memory_space=pltpu.VMEM),
         scratch_shapes=[
             pltpu.VMEM(arrived.shape, jnp.bfloat16),
             pltpu.VMEM(gate_up.shape, jnp.bfloat16),
             pltpu.VMEM(down.shape, jnp.bfloat16),
             pltpu.VMEM((live_rows, feat_width), jnp.bfloat16),
             pltpu.VMEM((live_rows, hidden_width), jnp.bfloat16),
-            pltpu.VMEM((SLOTS, block_rows, group_width), jnp.bfloat16),
             pltpu.SemaphoreType.DMA((runs,)),
             pltpu.SemaphoreType.DMA((tiles,)),
             pltpu.SemaphoreType.DMA((ROWS,)),
-            pltpu.SemaphoreType.DMA((SLOTS,)),
         ],
-        compiler_params=pltpu.CompilerParams(vmem_limit_bytes=56 * MIB),
+        compiler_params=pltpu.CompilerParams(vmem_limit_bytes=48 * MIB),
         cost_estimate=pl.CostEstimate(
             flops=2 * live_rows * 3 * feat_width * hidden_width,
             bytes_accessed=6 * feat_width * hidden_width + 4 * block_rows * packed_width,
@@ -311,44 +308,15 @@
     )(*(pltpu.with_memory_space_constraint(a, pltpu.HBM) for a in (arrived, gate_up, down)))
 
 
-def combine_kernel(
-    slot_given_ref, mix_given_ref, given_ref, out_ref,
-    slot_ref, mix_ref, in_ref, weight_ref, slot_sem, mix_sem, in_sem,
-):
+def combine_kernel(weight_ref, in_ref, out_ref):
     tok_rows, feat_width = out_ref.shape
     group_width = feat_width // ROWS
 
     def group(g):
         return slice(g * group_width, (g + 1) * group_width)
 
-    plans = [
-        pltpu.make_async_copy(slot_given_ref, slot_ref, slot_sem),
-        pltpu.make_async_copy(mix_given_ref, mix_ref, mix_sem),
-    ]
-    reads = [
-        pltpu.make_async_copy(given_ref.at[:, group(g)], in_ref.at[:, group(g)], in_sem.at[g])
-        for g in range(SLOTS)
-    ]
-    for copy in plans + reads[:AHEAD]:
-        copy.start()
-    for copy in plans:
-        copy.wait()
-    slot, mix = slot_ref[...], mix_ref[...]
-    row = iota(slot.shape, 1) % ROWS
-    own = jnp.where((row < SLOTS) & (slot == row.astype(jnp.float32)), mix, 0.0)
-    own = own.astype(weight_ref.dtype)
-    for g in range(SLOTS):
-        weight_ref[g, :tok_rows] = own
-        here = jnp.where(slot == float(g), mix, 0.0)
-        for i in range(EXTRA):
-            weight_ref[g, (1 + i) * tok_rows : (2 + i) * tok_rows] = jnp.where(
-                row == SLOTS + i, here, 0.0
-            ).astype(weight_ref.dtype)
     total = jnp.zeros((EXTRA * tok_rows, group_width), jnp.float32)
     for g in range(SLOTS):
-        reads[g].wait()
-        for copy in reads[g + AHEAD : g + AHEAD + 1]:
-            copy.start()
         part = jnp.dot(weight_ref[g], in_ref[:, group(g)], preferred_element_type=jnp.float32)
         out_ref[:, group(g)] = part[:tok_rows].astype(out_ref.dtype)
         total = total + part[tok_rows:]
@@ -356,26 +324,16 @@
         out_ref[:, group(SLOTS + i)] = total[i * tok_rows : (i + 1) * tok_rows].astype(out_ref.dtype)
 
 
-def combine(planned, returned, out_shape):
-    slot, mix = planned
-    given = pl.BlockSpec(memory_space=pl.ANY)
+def combine(weights, returned, out_shape):
+    held = pl.BlockSpec(memory_space=pltpu.VMEM)
     return pl.pallas_call(
         combine_kernel,
         out_shape=out_shape,
-        in_specs=[given, given, given],
-        out_specs=pl.BlockSpec(memory_space=pltpu.VMEM),
-        scratch_shapes=[
-            pltpu.VMEM(slot.shape, slot.dtype),
-            pltpu.VMEM(mix.shape, mix.dtype),
-            pltpu.VMEM(returned.shape, returned.dtype),
-            pltpu.VMEM((SLOTS, (1 + EXTRA) * out_shape.shape[0], slot.shape[1]), jnp.bfloat16),
-            pltpu.SemaphoreType.DMA,
-            pltpu.SemaphoreType.DMA,
-            pltpu.SemaphoreType.DMA((SLOTS,)),
-        ],
-        compiler_params=pltpu.CompilerParams(vmem_limit_bytes=32 * MIB),
+        in_specs=[held, held],
+        out_specs=held,
+        compiler_params=pltpu.CompilerParams(vmem_limit_bytes=24 * MIB),
         name="combine",
-    )(*(pltpu.with_memory_space_constraint(a, pltpu.HBM) for a in (slot, mix, returned)))
+    )(*(pltpu.with_memory_space_constraint(a, pltpu.VMEM) for a in (weights, returned)))
 
 
 def exchange(blocks, experts):
@@ -404,6 +362,7 @@
     gate_up = dequant(w_gate_up[0], gu_scales[0], 256, place)
     down = dequant(w_down[0], down_scales[0], 128, lambda j: j)
     planned = plan(expert_ids, gate_weights, experts)
+    arrived, planned = lax.optimization_barrier((arrived, planned))
     returned = exchange(expert(arrived, gate_up, down, tile), experts)
     return combine(planned, returned, jax.ShapeDtypeStruct(tokens.shape, tokens.dtype))
 

time: 180 us -> 175 us (0.972)
  blocking collectives: 0 us -> 68.8 us
  waiting for transfers between devices: 98 us -> 32.7 us
  starting transfers between devices: 17.5 us -> 11.9 us
  Pallas kernels: 63 us -> 60.5 us
    all_to_all x0 -> x1, blocking collectives: none -> 68.8 us  [exchange(): lax.all_to_all(blocks.reshape(experts, ROWS, shape[1]), ('expert', 'helpe...]
    all_to_all x2 -> x1, waiting for transfers between devices: 98 us -> 32.7 us  [exchange(): lax.all_to_all(blocks.reshape(experts, ROWS, shape[1]), ('expert', 'helpe...]
    all_to_all x2 -> x1, starting transfers between devices: 17.5 us -> 11.9 us  [exchange(): lax.all_to_all(blocks.reshape(experts, ROWS, shape[1]), ('expert', 'helpe...]
  transfers between devices with their start and end apart: 2 -> 1, of which waited for: 2 -> 1; matrix products, arithmetic and copies ran while one was open for 0% -> 0% of each run, Pallas kernels for 17% -> 18%
where the time goes in v3:
time: 175 us; the launch traced here: 174 us
  blocking collectives  68.8 us (39%)
  Pallas kernels  60.5 us (35%)
  waiting for transfers between devices  32.7 us (19%)
  starting transfers between devices  11.9 us (7%)
    all_to_all x1, blocking collectives, exchange(): lax.all_to_all(blocks.reshape(experts, ROWS, shape[1]), ('expert', 'helpe...  68.8 us
    all_to_all x1, waiting for transfers between devices, exchange(): lax.all_to_all(blocks.reshape(experts, ROWS, shape[1]), ('expert', 'helpe...  32.7 us
    pallas_call x2, Pallas kernels, dequant(): pl.pallas_call(functools.partial(dequant_kernel, place), grid=(row_count...  28.6 us
    pallas_call x1, Pallas kernels, expert(): pl.pallas_call(functools.partial(expert_kernel, hidden_tile), out_shape=p...  22.9 us
    all_to_all x1, starting transfers between devices, exchange(): lax.all_to_all(blocks.reshape(experts, ROWS, shape[1]), ('expert', 'helpe...  11.9 us
    pallas_call x1, Pallas kernels, pack(): pl.pallas_call(pack_kernel, out_shape=pltpu.HBM(shape, tokens.dtype), in_...  4.17 us
  transfers between devices with their start and end apart: 1, of which 1 were waited for; matrix products, arithmetic and copies ran while one was open for 0% of the time, Pallas kernels for 18%

profile of v3, /device:TPU:1, one launch (start us, length us, event | category | flops | bytes accessed | tf_op | source)
XLA Modules:
  0.0 174.3 jit_solution(13823331696386556639)
XLA Ops:
  0.0 4.2 %pack.1 = bf16[1024,2560]{1,0:T(8,128)(2,1)} custom-call(s32[8,64]{1,0:T(8,128)} %bitcast.16, bf16[64,4096]{1,0:T(8,128)(2,1)} %given_ref.1), custom_call_target="tpu_custom_call" | custom-call | tf_op jit(solution)/shard_map/pack/pallas_call | solution.py:103
  4.2 0.0 copy-start.2
  4.2 0.0 copy-start.3
  4.2 0.0 copy-start.4
  4.2 0.0 copy-start.1
  4.2 11.9 %all-to-all-start = ((bf16[128,8,2560]{2,1,0:T(8,128)(2,1)}), bf16[128,8,2560]{2,1,0:T(8,128)(2,1)}, u32[]{:S(2)}, u32[]{:S(2)}) async-start(bf16[128,8,2560]{2,1,0:T(8,128)(2,1)} %bitcast.13), calls=%async_computation | async-start | bytes 10485760 | tf_op jit(solution)/shard_map/all_to_all | solution.py:341
  16.1 0.0 copy-done.2
  16.1 0.1 copy.8.ids_ref
  16.2 0.0 copy-done.3
  16.2 0.1 copy.10
  16.3 0.0 copy-done.4
  16.3 0.1 copy.9.gate_ref
  16.4 0.0 copy-done.1
  16.4 9.7 %dequant.3.down_given_ref = bf16[1024,4096]{1,0:T(8,128)(2,1)} custom-call(f32[8,32]{1,0:T(8,128)S(1)} %bitcast.12, bf16[1024,4096]{1,0:T(8,128)(2,1)} %bitcast.15), custom_call_target="tpu_custom_call" | custom-call | flops 4194304 | bytes 16777216 | tf_op jit(solution)/shard_map/dequant/pallas_call | solution.py:175
  26.1 18.9 %dequant.2.gu_given_ref = bf16[4096,2048]{1,0:T(8,128)(2,1)} custom-call(f32[32,16]{1,0:T(8,128)S(1)} %bitcast.11, bf16[4096,2048]{1,0:T(8,128)(2,1)} %bitcast.14), custom_call_target="tpu_custom_call" | custom-call | flops 8388608 | bytes 33554432 | tf_op jit(solution)/shard_map/dequant/pallas_call | solution.py:175
  45.0 2.5 %plan.1.weight_ref = bf16[5,256,1024]{2,1,0:T(8,128)(2,1)} custom-call(s32[64,8]{1,0:T(8,128)S(1)} %copy.8.ids_ref, f32[64,8]{1,0:T(8,128)S(1)} %copy.9.gate_ref), custom_call_target="tpu_custom_call" | custom-call | flops 100000000 | bytes 1000000 | tf_op jit(solution)/shard_map/plan/pallas_call | solution.py:152
  47.5 32.7 %all-to-all-done = bf16[128,8,2560]{2,1,0:T(8,128)(2,1)} async-done(((bf16[128,8,2560]{2,1,0:T(8,128)(2,1)}), bf16[128,8,2560]{2,1,0:T(8,128)(2,1)}, u32[]{:S(2)}, u32[]{:S(2)}) %all-to-all-start) | async-done | bytes 5242912 | tf_op jit(solution)/shard_map/all_to_all | solution.py:341
  80.2 22.9 %expert.1 = bf16[1024,2560]{1,0:T(8,128)(2,1)S(1)} custom-call(bf16[1024,2560]{1,0:T(8,128)(2,1)} %bitcast.2.given_ref, bf16[4096,2048]{1,0:T(8,128)(2,1)} %dequant.2.gu_given_ref, bf16[1024,4096]{1,0:T(8,128)(2,1)} %dequant.3.down_given_ref), custom_call_target="tpu_custom_call" | custom-call | flops 16106127360 | bytes 35651584 | tf_op jit(solution)/shard_map/expert/pallas_call | solution.py:286
  103.1 0.0 copy-start
  103.1 68.8 %all_to_all.10 = bf16[128,8,2560]{2,1,0:T(8,128)(2,1)S(1)} all-to-all(bf16[128,8,2560]{2,1,0:T(8,128)(2,1)S(1)} %bitcast.10), channel_id=1, replica_groups=mesh['expert'=16,'helper'=8] {'expert','helper'}, dimensions={0} | all-to-all | bytes 10485760 | tf_op jit(solution)/shard_map/all_to_all | solution.py:341
  171.9 0.0 copy-done
  171.9 2.3 %combine.1 = bf16[64,4096]{1,0:T(8,128)(2,1)} custom-call(bf16[5,256,1024]{2,1,0:T(8,128)(2,1)S(1)} %copy-done, bf16[1024,2560]{1,0:T(8,128)(2,1)S(1)} %bitcast.9), custom_call_target="tpu_custom_call" | custom-call | tf_op jit(solution)/shard_map/combine/pallas_call | solution.py:329
Async XLA Ops:
  4.2 12.0 %copy-start.2 = (s32[64,8]{0,1:T(8,128)S(1)}, s32[64,8]{0,1:T(8,128)}, u32[]{:S(2)}) copy-start(s32[64,8]{0,1:T(8,128)} %param.8) | copy-start | bytes 6148
  4.2 12.0 %copy-start.3 = (f32[1,32,16]{1,2,0:T(8,128)S(1)}, f32[1,32,16]{1,2,0:T(8,128)}, u32[]{:S(2)}) copy-start(f32[1,32,16]{1,2,0:T(8,128)} %param.11) | copy-start | bytes 6148
  4.2 12.1 %copy-start.4 = (f32[64,8]{0,1:T(8,128)S(1)}, f32[64,8]{0,1:T(8,128)}, u32[]{:S(2)}) copy-start(f32[64,8]{0,1:T(8,128)} %param.9) | copy-start | bytes 6148
  4.2 12.2 %copy-start.1 = (f32[1,8,32]{2,1,0:T(8,128)S(1)}, f32[1,8,32]{2,1,0:T(8,128)}, u32[]{:S(2)}) copy-start(f32[1,8,32]{2,1,0:T(8,128)} %param.13) | copy-start | bytes 3076
  4.2 76.0 %all-to-all-start = ((bf16[128,8,2560]{2,1,0:T(8,128)(2,1)}), bf16[128,8,2560]{2,1,0:T(8,128)(2,1)}, u32[]{:S(2)}, u32[]{:S(2)}) async-start(bf16[128,8,2560]{2,1,0:T(8,128)(2,1)} %bitcast.13), calls=%async_computation | async-start | bytes 10485760 | tf_op jit(solution)/shard_map/all_to_all | solution.py:341
  103.1 68.8 %copy-start = (bf16[5,256,1024]{2,1,0:T(8,128)(2,1)S(1)}, bf16[5,256,1024]{2,1,0:T(8,128)(2,1)}, u32[]{:S(2)}) copy-start(bf16[5,256,1024]{2,1,0:T(8,128)(2,1)} %plan.1.weight_ref) | copy-start | bytes 7864324

commit v4 on v3

--- a/solution.py
+++ b/solution.py
@@ -239,7 +239,8 @@
             copy.start()
         pre = jnp.dot(x_ref[...], gu_ref[gu_places[tile]], preferred_element_type=jnp.float32)
         gate, up = pre[:, :hidden_tile], pre[:, hidden_tile:]
-        hidden_ref[:, run_rows(tile, hidden_tile)] = (gate / (1.0 + jnp.exp(-gate)) * up).astype(
+        half = 0.5 * gate
+        hidden_ref[:, run_rows(tile, hidden_tile)] = (half * (1.0 + jnp.tanh(half)) * up).astype(
             hidden_ref.dtype
         )
     pack_again = turned(True)

time: 175 us -> 175 us (level)
  no operation moved by 1% of the time
where the time goes in v4:
time: 175 us; the launch traced here: 174 us
  blocking collectives  68.8 us (39%)
  Pallas kernels  60.4 us (35%)
  waiting for transfers between devices  32.7 us (19%)
  starting transfers between devices  11.9 us (7%)
    all_to_all x1, blocking collectives, exchange(): lax.all_to_all(blocks.reshape(experts, ROWS, shape[1]), ('expert', 'helpe...  68.8 us
    all_to_all x1, waiting for transfers between devices, exchange(): lax.all_to_all(blocks.reshape(experts, ROWS, shape[1]), ('expert', 'helpe...  32.7 us
    pallas_call x2, Pallas kernels, dequant(): pl.pallas_call(functools.partial(dequant_kernel, place), grid=(row_count...  28.6 us
    pallas_call x1, Pallas kernels, expert(): pl.pallas_call(functools.partial(expert_kernel, hidden_tile), out_shape=p...  22.8 us
    all_to_all x1, starting transfers between devices, exchange(): lax.all_to_all(blocks.reshape(experts, ROWS, shape[1]), ('expert', 'helpe...  11.9 us
    pallas_call x1, Pallas kernels, pack(): pl.pallas_call(pack_kernel, out_shape=pltpu.HBM(shape, tokens.dtype), in_...  4.17 us
  transfers between devices with their start and end apart: 1, of which 1 were waited for; matrix products, arithmetic and copies ran while one was open for 0% of the time, Pallas kernels for 18%

profile of v4, /device:TPU:1, one launch (start us, length us, event | category | flops | bytes accessed | tf_op | source)
XLA Modules:
  0.0 174.2 jit_solution(12805972739561157634)
XLA Ops:
  0.0 4.2 %pack.1 = bf16[1024,2560]{1,0:T(8,128)(2,1)} custom-call(s32[8,64]{1,0:T(8,128)} %bitcast.16, bf16[64,4096]{1,0:T(8,128)(2,1)} %given_ref.1), custom_call_target="tpu_custom_call" | custom-call | tf_op jit(solution)/shard_map/pack/pallas_call | solution.py:103
  4.2 0.0 copy-start.2
  4.2 0.0 copy-start.3
  4.2 0.0 copy-start.4
  4.2 0.0 copy-start.1
  4.2 11.9 %all-to-all-start = ((bf16[128,8,2560]{2,1,0:T(8,128)(2,1)}), bf16[128,8,2560]{2,1,0:T(8,128)(2,1)}, u32[]{:S(2)}, u32[]{:S(2)}) async-start(bf16[128,8,2560]{2,1,0:T(8,128)(2,1)} %bitcast.13), calls=%async_computation | async-start | bytes 10485760 | tf_op jit(solution)/shard_map/all_to_all | solution.py:342
  16.1 0.0 copy-done.2
  16.1 0.1 copy.8.ids_ref
  16.2 0.0 copy-done.3
  16.2 0.1 copy.10
  16.3 0.0 copy-done.4
  16.3 0.1 copy.9.gate_ref
  16.4 0.0 copy-done.1
  16.4 9.7 %dequant.3.down_given_ref = bf16[1024,4096]{1,0:T(8,128)(2,1)} custom-call(f32[8,32]{1,0:T(8,128)S(1)} %bitcast.12, bf16[1024,4096]{1,0:T(8,128)(2,1)} %bitcast.15), custom_call_target="tpu_custom_call" | custom-call | flops 4194304 | bytes 16777216 | tf_op jit(solution)/shard_map/dequant/pallas_call | solution.py:175
  26.1 18.9 %dequant.2.gu_given_ref = bf16[4096,2048]{1,0:T(8,128)(2,1)} custom-call(f32[32,16]{1,0:T(8,128)S(1)} %bitcast.11, bf16[4096,2048]{1,0:T(8,128)(2,1)} %bitcast.14), custom_call_target="tpu_custom_call" | custom-call | flops 8388608 | bytes 33554432 | tf_op jit(solution)/shard_map/dequant/pallas_call | solution.py:175
  45.0 2.5 %plan.1.weight_ref = bf16[5,256,1024]{2,1,0:T(8,128)(2,1)} custom-call(s32[64,8]{1,0:T(8,128)S(1)} %copy.8.ids_ref, f32[64,8]{1,0:T(8,128)S(1)} %copy.9.gate_ref), custom_call_target="tpu_custom_call" | custom-call | flops 100000000 | bytes 1000000 | tf_op jit(solution)/shard_map/plan/pallas_call | solution.py:152
  47.5 32.7 %all-to-all-done = bf16[128,8,2560]{2,1,0:T(8,128)(2,1)} async-done(((bf16[128,8,2560]{2,1,0:T(8,128)(2,1)}), bf16[128,8,2560]{2,1,0:T(8,128)(2,1)}, u32[]{:S(2)}, u32[]{:S(2)}) %all-to-all-start) | async-done | bytes 5242912 | tf_op jit(solution)/shard_map/all_to_all | solution.py:342
  80.2 22.8 %expert.1 = bf16[1024,2560]{1,0:T(8,128)(2,1)S(1)} custom-call(bf16[1024,2560]{1,0:T(8,128)(2,1)} %bitcast.2.given_ref, bf16[4096,2048]{1,0:T(8,128)(2,1)} %dequant.2.gu_given_ref, bf16[1024,4096]{1,0:T(8,128)(2,1)} %dequant.3.down_given_ref), custom_call_target="tpu_custom_call" | custom-call | flops 16106127360 | bytes 35651584 | tf_op jit(solution)/shard_map/expert/pallas_call | solution.py:287
  103.1 0.0 copy-start
  103.1 68.8 %all_to_all.10 = bf16[128,8,2560]{2,1,0:T(8,128)(2,1)S(1)} all-to-all(bf16[128,8,2560]{2,1,0:T(8,128)(2,1)S(1)} %bitcast.10), channel_id=1, replica_groups=mesh['expert'=16,'helper'=8] {'expert','helper'}, dimensions={0} | all-to-all | bytes 10485760 | tf_op jit(solution)/shard_map/all_to_all | solution.py:342
  171.9 0.0 copy-done
  171.9 2.3 %combine.1 = bf16[64,4096]{1,0:T(8,128)(2,1)} custom-call(bf16[5,256,1024]{2,1,0:T(8,128)(2,1)S(1)} %copy-done, bf16[1024,2560]{1,0:T(8,128)(2,1)S(1)} %bitcast.9), custom_call_target="tpu_custom_call" | custom-call | tf_op jit(solution)/shard_map/combine/pallas_call | solution.py:330
Async XLA Ops:
  4.2 12.0 %copy-start.2 = (s32[64,8]{0,1:T(8,128)S(1)}, s32[64,8]{0,1:T(8,128)}, u32[]{:S(2)}) copy-start(s32[64,8]{0,1:T(8,128)} %param.8) | copy-start | bytes 6148
  4.2 12.0 %copy-start.3 = (f32[1,32,16]{1,2,0:T(8,128)S(1)}, f32[1,32,16]{1,2,0:T(8,128)}, u32[]{:S(2)}) copy-start(f32[1,32,16]{1,2,0:T(8,128)} %param.11) | copy-start | bytes 6148
  4.2 12.1 %copy-start.4 = (f32[64,8]{0,1:T(8,128)S(1)}, f32[64,8]{0,1:T(8,128)}, u32[]{:S(2)}) copy-start(f32[64,8]{0,1:T(8,128)} %param.9) | copy-start | bytes 6148
  4.2 12.2 %copy-start.1 = (f32[1,8,32]{2,1,0:T(8,128)S(1)}, f32[1,8,32]{2,1,0:T(8,128)}, u32[]{:S(2)}) copy-start(f32[1,8,32]{2,1,0:T(8,128)} %param.13) | copy-start | bytes 3076
  4.2 76.0 %all-to-all-start = ((bf16[128,8,2560]{2,1,0:T(8,128)(2,1)}), bf16[128,8,2560]{2,1,0:T(8,128)(2,1)}, u32[]{:S(2)}, u32[]{:S(2)}) async-start(bf16[128,8,2560]{2,1,0:T(8,128)(2,1)} %bitcast.13), calls=%async_computation | async-start | bytes 10485760 | tf_op jit(solution)/shard_map/all_to_all | solution.py:342
  103.1 68.8 %copy-start = (bf16[5,256,1024]{2,1,0:T(8,128)(2,1)S(1)}, bf16[5,256,1024]{2,1,0:T(8,128)(2,1)}, u32[]{:S(2)}) copy-start(bf16[5,256,1024]{2,1,0:T(8,128)(2,1)} %plan.1.weight_ref) | copy-start | bytes 7864324

commit v5 on v4

--- a/solution.py
+++ b/solution.py
@@ -44,7 +44,7 @@
     return jnp.where(hit > 0.5, rank, -1.0)
 
 
-ALWAYS = 99.0
+ALWAYS, SHARED, NEVER = 99.0, -2, -3
 
 
 def pack_kernel(
@@ -59,21 +59,25 @@
     fetch_ids.start()
     fetch = pltpu.make_async_copy(given_ref, tok_ref, tok_sem)
     fetch.start()
-    fetch_ids.wait()
-
-    slot = slots_for(ids_ref[...], experts).astype(jnp.bfloat16)
     repeat = jnp.where(
         iota((block_rows, experts), 0) // ROWS == iota((block_rows, experts), 1), 1.0, 0.0
     ).astype(jnp.bfloat16)
-    spread = jnp.dot(
-        repeat, jnp.concatenate([slot] * parts, axis=1), preferred_element_type=jnp.float32
-    )
     shape = (block_rows, parts * tok_rows)
     row = iota(shape, 0) % ROWS
     part = iota(shape, 1) // tok_rows
-    own = (part == 0) & (row.astype(jnp.float32) == spread) & (row < SLOTS)
+    own = (part == 0) & (row < SLOTS)
     shared = (part > 0) & (row == SLOTS - 1 + part)
-    slot_ref[...] = jnp.where(own, ALWAYS, jnp.where(shared, spread, -1.0))
+    slot_ref[...] = jnp.where(own, row, jnp.where(shared, SHARED, NEVER)).astype(jnp.float32)
+
+    fetch_ids.wait()
+    slot = slots_for(ids_ref[...], experts).astype(jnp.bfloat16)
+    spread = jnp.dot(
+        repeat, jnp.concatenate([slot] * parts, axis=1), preferred_element_type=jnp.float32
+    )
+    wanted = slot_ref[...]
+    slot_ref[...] = jnp.where(
+        wanted == spread, ALWAYS, jnp.where(wanted == float(SHARED), spread, -1.0)
+    )
     fetch.wait()
 
     def group(g):
@@ -263,17 +267,20 @@
                 pack_again, gathered, preferred_element_type=jnp.float32
             ).astype(out_ref.dtype)
 
-    for copy in down_copies[:EXTRA + 1]:
+    for copy in down_copies[: EXTRA + 1]:
         copy.wait()
     result = product(SLOTS - 1, EXTRA + 1)
     x_ref[:, SLOTS * group_width :] = result[:, group_width:]
-    give(SLOTS - 1, result[:, :group_width])
+    held = [(SLOTS - 1, result[:, :group_width])]
     for copy in down_copies[EXTRA + 1 :]:
         copy.wait()
     for feature in range(0, SLOTS - 1, 2):
         result = product(feature, 2)
-        give(feature, result[:, :group_width])
-        give(feature + 1, result[:, group_width:])
+        for done in held:
+            give(*done)
+        held = [(feature, result[:, :group_width]), (feature + 1, result[:, group_width:])]
+    for done in held:
+        give(*done)
 
 
 def expert(arrived, gate_up, down, hidden_tile):

time: 175 us -> 175 us (level)
  no operation moved by 1% of the time
where the time goes in v5:
time: 175 us; the launch traced here: 174 us
  blocking collectives  68.8 us (39%)
  Pallas kernels  60.4 us (35%)
  waiting for transfers between devices  32.7 us (19%)
  starting transfers between devices  11.9 us (7%)
    all_to_all x1, blocking collectives, exchange(): lax.all_to_all(blocks.reshape(experts, ROWS, shape[1]), ('expert', 'helpe...  68.8 us
    all_to_all x1, waiting for transfers between devices, exchange(): lax.all_to_all(blocks.reshape(experts, ROWS, shape[1]), ('expert', 'helpe...  32.7 us
    pallas_call x2, Pallas kernels, dequant(): pl.pallas_call(functools.partial(dequant_kernel, place), grid=(row_count...  28.6 us
    pallas_call x1, Pallas kernels, expert(): pl.pallas_call(functools.partial(expert_kernel, hidden_tile), out_shape=p...  22.8 us
    all_to_all x1, starting transfers between devices, exchange(): lax.all_to_all(blocks.reshape(experts, ROWS, shape[1]), ('expert', 'helpe...  11.9 us
    pallas_call x1, Pallas kernels, pack(): pl.pallas_call(pack_kernel, out_shape=pltpu.HBM(shape, tokens.dtype), in_...  4.13 us
  transfers between devices with their start and end apart: 1, of which 1 were waited for; matrix products, arithmetic and copies ran while one was open for 0% of the time, Pallas kernels for 18%

profile of v5, /device:TPU:1, one launch (start us, length us, event | category | flops | bytes accessed | tf_op | source)
XLA Modules:
  0.0 174.2 jit_solution(700733428247157897)
XLA Ops:
  0.0 4.1 %pack.1 = bf16[1024,2560]{1,0:T(8,128)(2,1)} custom-call(s32[8,64]{1,0:T(8,128)} %bitcast.16, bf16[64,4096]{1,0:T(8,128)(2,1)} %given_ref.1), custom_call_target="tpu_custom_call" | custom-call | tf_op jit(solution)/shard_map/pack/pallas_call | solution.py:107
  4.1 0.0 copy-start.2
  4.2 0.0 copy-start.3
  4.2 0.0 copy-start.4
  4.2 0.0 copy-start.1
  4.2 11.9 %all-to-all-start = ((bf16[128,8,2560]{2,1,0:T(8,128)(2,1)}), bf16[128,8,2560]{2,1,0:T(8,128)(2,1)}, u32[]{:S(2)}, u32[]{:S(2)}) async-start(bf16[128,8,2560]{2,1,0:T(8,128)(2,1)} %bitcast.13), calls=%async_computation | async-start | bytes 10485760 | tf_op jit(solution)/shard_map/all_to_all | solution.py:349
  16.1 0.0 copy-done.2
  16.1 0.1 copy.8.ids_ref
  16.2 0.0 copy-done.3
  16.2 0.1 copy.10
  16.3 0.0 copy-done.4
  16.3 0.1 copy.9.gate_ref
  16.4 0.0 copy-done.1
  16.4 9.7 %dequant.3.down_given_ref = bf16[1024,4096]{1,0:T(8,128)(2,1)} custom-call(f32[8,32]{1,0:T(8,128)S(1)} %bitcast.12, bf16[1024,4096]{1,0:T(8,128)(2,1)} %bitcast.15), custom_call_target="tpu_custom_call" | custom-call | flops 4194304 | bytes 16777216 | tf_op jit(solution)/shard_map/dequant/pallas_call | solution.py:179
  26.1 18.9 %dequant.2.gu_given_ref = bf16[4096,2048]{1,0:T(8,128)(2,1)} custom-call(f32[32,16]{1,0:T(8,128)S(1)} %bitcast.11, bf16[4096,2048]{1,0:T(8,128)(2,1)} %bitcast.14), custom_call_target="tpu_custom_call" | custom-call | flops 8388608 | bytes 33554432 | tf_op jit(solution)/shard_map/dequant/pallas_call | solution.py:179
  45.0 2.5 %plan.1.weight_ref = bf16[5,256,1024]{2,1,0:T(8,128)(2,1)} custom-call(s32[64,8]{1,0:T(8,128)S(1)} %copy.8.ids_ref, f32[64,8]{1,0:T(8,128)S(1)} %copy.9.gate_ref), custom_call_target="tpu_custom_call" | custom-call | flops 100000000 | bytes 1000000 | tf_op jit(solution)/shard_map/plan/pallas_call | solution.py:156
  47.5 32.7 %all-to-all-done = bf16[128,8,2560]{2,1,0:T(8,128)(2,1)} async-done(((bf16[128,8,2560]{2,1,0:T(8,128)(2,1)}), bf16[128,8,2560]{2,1,0:T(8,128)(2,1)}, u32[]{:S(2)}, u32[]{:S(2)}) %all-to-all-start) | async-done | bytes 5242912 | tf_op jit(solution)/shard_map/all_to_all | solution.py:349
  80.2 22.8 %expert.1 = bf16[1024,2560]{1,0:T(8,128)(2,1)S(1)} custom-call(bf16[1024,2560]{1,0:T(8,128)(2,1)} %bitcast.2.given_ref, bf16[4096,2048]{1,0:T(8,128)(2,1)} %dequant.2.gu_given_ref, bf16[1024,4096]{1,0:T(8,128)(2,1)} %dequant.3.down_given_ref), custom_call_target="tpu_custom_call" | custom-call | flops 16106127360 | bytes 35651584 | tf_op jit(solution)/shard_map/expert/pallas_call | solution.py:294
  103.0 0.0 copy-start
  103.0 68.8 %all_to_all.10 = bf16[128,8,2560]{2,1,0:T(8,128)(2,1)S(1)} all-to-all(bf16[128,8,2560]{2,1,0:T(8,128)(2,1)S(1)} %bitcast.10), channel_id=1, replica_groups=mesh['expert'=16,'helper'=8] {'expert','helper'}, dimensions={0} | all-to-all | bytes 10485760 | tf_op jit(solution)/shard_map/all_to_all | solution.py:349
  171.8 0.0 copy-done
  171.8 2.3 %combine.1 = bf16[64,4096]{1,0:T(8,128)(2,1)} custom-call(bf16[5,256,1024]{2,1,0:T(8,128)(2,1)S(1)} %copy-done, bf16[1024,2560]{1,0:T(8,128)(2,1)S(1)} %bitcast.9), custom_call_target="tpu_custom_call" | custom-call | tf_op jit(solution)/shard_map/combine/pallas_call | solution.py:337
Async XLA Ops:
  4.1 12.0 %copy-start.2 = (s32[64,8]{0,1:T(8,128)S(1)}, s32[64,8]{0,1:T(8,128)}, u32[]{:S(2)}) copy-start(s32[64,8]{0,1:T(8,128)} %param.8) | copy-start | bytes 6148
  4.2 12.0 %copy-start.3 = (f32[1,32,16]{1,2,0:T(8,128)S(1)}, f32[1,32,16]{1,2,0:T(8,128)}, u32[]{:S(2)}) copy-start(f32[1,32,16]{1,2,0:T(8,128)} %param.11) | copy-start | bytes 6148
  4.2 12.1 %copy-start.4 = (f32[64,8]{0,1:T(8,128)S(1)}, f32[64,8]{0,1:T(8,128)}, u32[]{:S(2)}) copy-start(f32[64,8]{0,1:T(8,128)} %param.9) | copy-start | bytes 6148
  4.2 12.2 %copy-start.1 = (f32[1,8,32]{2,1,0:T(8,128)S(1)}, f32[1,8,32]{2,1,0:T(8,128)}, u32[]{:S(2)}) copy-start(f32[1,8,32]{2,1,0:T(8,128)} %param.13) | copy-start | bytes 3076
  4.2 76.0 %all-to-all-start = ((bf16[128,8,2560]{2,1,0:T(8,128)(2,1)}), bf16[128,8,2560]{2,1,0:T(8,128)(2,1)}, u32[]{:S(2)}, u32[]{:S(2)}) async-start(bf16[128,8,2560]{2,1,0:T(8,128)(2,1)} %bitcast.13), calls=%async_computation | async-start | bytes 10485760 | tf_op jit(solution)/shard_map/all_to_all | solution.py:349
  103.0 68.8 %copy-start = (bf16[5,256,1024]{2,1,0:T(8,128)(2,1)S(1)}, bf16[5,256,1024]{2,1,0:T(8,128)(2,1)}, u32[]{:S(2)}) copy-start(bf16[5,256,1024]{2,1,0:T(8,128)(2,1)} %plan.1.weight_ref) | copy-start | bytes 7864324
